TPU v7x, 256 devices: a whole 4x4x8 slice. The times are simulated.
256 devices in a mesh: dp: 8 (over z_lo, core), expert: 32 (over y, z_hi, x).
Axes of the slice: x: 4, y: 4, z: 8 (z_hi: 2, z_lo: 4; z = z_hi * 4 + z_lo), core: 2. Of those that a mesh axis runs over, the one named last changes fastest.
Arguments:
- tokens: bfloat16 [2, 1024, 7168], P(None, 'dp'), may hold values from -6 to 6
- scores: float32 [2, 1024, 8], P(None, 'dp'), may hold values from 0.05 to 1
- expert_ids: int32 [2, 1024, 8], P(None, 'dp'), may hold values from 0 to 31, all different within a row; in each aligned block of 128 rows (0 to 127, 128 to 255, ..., all dimensions but the last counted through in order) at most 48 rows name the same one
- slot_expert: int32 [32], replicated, may hold values from 0 to 31, each once
- w_gate: bfloat16 [32, 7168, 1024], P('expert', 'dp'), may hold values from -0.0625 to 0.0625
- w_up: bfloat16 [32, 7168, 1024], P('expert', 'dp'), may hold values from -0.0625 to 0.0625
- w_down: bfloat16 [32, 1024, 7168], P('expert', None, 'dp'), may hold values from -0.1875 to 0.1875
Outputs:
- mixed: bfloat16 [2, 1024, 7168], P(None, ('dp', 'expert'))
Inputs may be any that keep to these rules, and one draw needn't show every extreme that they name: `expert_ids`: each token names 8 different experts. In each micro-batch the 128 tokens on one index of dp name any one expert at most 48 times; some of these blocks reach the bound. `slot_expert`: each expert stands in exactly one slot.
All inputs are finite; a program needn't handle non-finite values.
Results may differ from a plain program's by a relative error of at most 0.0058.
Values may be sent and summed in bfloat16 or wider, within the bound.
A program may use at most 64 MiB of HBM per device.

v0:
```python
import jax
import jax.numpy as jnp
from jax import lax
from jax.sharding import PartitionSpec as P

ROUTE_SCALE = 2.5


def routing(scores, expert_ids, logical):
    weights = ROUTE_SCALE * scores / jnp.sum(scores, axis=-1, keepdims=True)
    matched = expert_ids == logical
    shares = jnp.sum(jnp.where(matched, weights, 0.0), axis=-1)
    present = jnp.any(matched, axis=-1).astype(jnp.int32)
    return (weights, shares, present)


def placement(present, capacity):
    ranked = jnp.cumsum(present) - present
    places = lax.broadcasted_iota(jnp.int32, (capacity, present.shape[0]), 0)
    chosen = (places == ranked[None, :]) & (present[None, :] > 0)
    return chosen.astype(jnp.bfloat16)


def per_device(tokens, scores, expert_ids, slot_expert, w_gate, w_up, w_down):
    experts_count = lax.axis_size("expert")
    groups = lax.axis_size("dp")
    batches = tokens.shape[0]
    tok_row = tokens.shape[1]
    model_width = tokens.shape[2]
    top_count = expert_ids.shape[2]
    capacity = 3 * tok_row * top_count // (2 * experts_count)
    piece_width = model_width // groups
    hidden_width = w_gate.shape[2]
    here = lax.axis_index("expert")
    logical = lax.dynamic_index_in_dim(slot_expert, here, 0, keepdims=False)
    gate_local = w_gate[0]
    up_local = w_up[0]
    down_local = w_down[0]

    def project_in(received):
        gate_sum = jnp.einsum(
            "rsd,dh->rsh", received, gate_local, preferred_element_type=jnp.float32
        )
        up_sum = jnp.einsum("rsd,dh->rsh", received, up_local, preferred_element_type=jnp.float32)
        return (gate_sum, up_sum)

    def project_out(piece):
        return jnp.dot(piece, down_local, preferred_element_type=jnp.float32)

    def expert_outputs(batch):
        weights, shares, present = routing(scores[batch], expert_ids[batch], logical)
        chooser = placement(present, capacity)
        packed = jnp.dot(chooser, tokens[batch], preferred_element_type=jnp.float32).astype(
            jnp.bfloat16
        )
        pieces = packed.reshape(capacity, groups, piece_width)
        gate_part, up_part = project_in(
            lax.all_to_all(pieces, "dp", split_axis=1, concat_axis=1, tiled=True)
        )
        gate_own, up_own = (
            lax.psum_scatter(gate_part, "dp", scatter_dimension=1, tiled=True),
            lax.psum_scatter(up_part, "dp", scatter_dimension=1, tiled=True),
        )
        hidden = (
            (jax.nn.silu(gate_own) * up_own).reshape(capacity, hidden_width).astype(jnp.bfloat16)
        )
        produced = project_out(lax.all_gather(hidden, "dp", axis=0, tiled=True))
        produced = produced.reshape(groups, capacity, piece_width)
        returned = lax.all_to_all(
            produced.astype(jnp.bfloat16), "dp", split_axis=0, concat_axis=2, tiled=True
        )
        return (weights, shares, chooser, returned.reshape(capacity, model_width))

    def combine(outcomes):
        weights = jnp.stack([outcome[0] for outcome in outcomes])
        shares = jnp.stack([outcome[1] for outcome in outcomes])
        chooser = jnp.stack([outcome[2] for outcome in outcomes])
        rows_out = jnp.stack([outcome[3] for outcome in outcomes])
        spread = jnp.einsum("kct,kcd->ktd", chooser, rows_out, preferred_element_type=jnp.float32)
        token_rows = lax.psum_scatter(
            shares[:, :, None] * spread, "expert", scatter_dimension=1, tiled=True
        )
        return token_rows.astype(jnp.bfloat16)

    finished = [combine([expert_outputs(batch)]) for batch in range(batches)]
    result = jnp.concatenate(finished, axis=0)
    return result


def solution(mesh):
    in_specs = (
        P(None, "dp", None),
        P(None, "dp", None),
        P(None, "dp", None),
        P(),
        P("expert", "dp", None),
        P("expert", "dp", None),
        P("expert", None, "dp"),
    )
    out_specs = P(None, ("dp", "expert"), None)
    return jax.shard_map(
        per_device, mesh=mesh, in_specs=in_specs, out_specs=out_specs, check_vma=False
    )
```

profile of v0, /device:TPU:33, one launch (start us, length us, event | category | flops | bytes accessed | tf_op | source)
XLA Modules:
  0.0 627.1 jit_solution(8860826342247619885)
XLA Ops:
  6.5 1.4 dynamic_slice.4
  7.9 1.3 fusion.42
  9.4 0.2 reduce-window.16
  9.7 1.9 convolution_convert_fusion.1
  11.6 22.6 %all_to_all.40 = bf16[48,8,896]{2,0,1:T(8,128)(2,1)S(1)} all-to-all(bf16[48,8,896]{2,0,1:T(8,128)(2,1)S(1)} %bitcast.96), channel_id=1, replica_groups=mesh['dp'=8,'expert'=32] {'dp'}, dimensions={1} | all-to-all | bytes 1376256 | tf_op jit(solution)/shard_map/all_to_all | solution.py:58
  34.2 2.1 fusion.13
  36.4 3.7 fusion.9
  40.2 0.7 fusion.40
  41.0 0.2 reduce-window.17
  41.3 1.9 convolution_convert_fusion
  43.3 28.9 %all_to_all.41 = bf16[48,8,896]{2,0,1:T(8,128)(2,1)S(1)} all-to-all(bf16[48,8,896]{2,0,1:T(8,128)(2,1)S(1)} %bitcast.97), channel_id=1, replica_groups=mesh['dp'=8,'expert'=32] {'dp'}, dimensions={1} | all-to-all | bytes 1376256 | tf_op jit(solution)/shard_map/all_to_all | solution.py:58
  72.1 2.1 fusion.11
  74.3 3.6 fusion.7
  78.0 7.0 %reduce-scatter.7.cloned.1.call-done = f32[48,1,1024]{2,0,1:T(8,128)} async-done(((f32[48,8,1024]{2,0,1:T(8,128)}), f32[48,1,1024]{2,0,1:T(8,128)}) %reduce-scatter.7.cloned.1.call-update) | async-done | bytes 196624 | tf_op jit(solution)/shard_map/reduce_scatter | solution.py:61
  85.0 35.4 %reduce-scatter.9.cloned.1.call-done = f32[48,1,1024]{2,0,1:T(8,128)} async-done(((f32[48,8,1024]{2,0,1:T(8,128)}), f32[48,1,1024]{2,0,1:T(8,128)}) %reduce-scatter.9.cloned.1.call-update) | async-done | bytes 196624 | tf_op jit(solution)/shard_map/reduce_scatter | solution.py:62
  120.4 1.1 multiply_convert_fusion.1
  121.4 19.9 %all-gather = bf16[384,1,1024]{2,0,1:T(8,128)(2,1)S(1)} all-gather(bf16[48,1,1024]{2,0,1:T(8,128)(2,1)S(1)} %multiply_convert_fusion.1), channel_id=2, replica_groups=mesh['dp'=8,'expert'=32] {'dp'}, dimensions={0}, use_global_device_ids=true | all-gather | bytes 884736 | tf_op jit(solution)/shard_map/all_gather | solution.py:67
  141.3 3.3 fusion.18
  144.7 6.6 %all-to-all-start.1 = ((bf16[8,48,896]{2,1,0:T(8,128)(2,1)}), bf16[8,48,896]{2,1,0:T(8,128)(2,1)S(1)}, u32[]{:S(2)}, u32[]{:S(2)}) async-start(bf16[8,48,896]{2,1,0:T(8,128)(2,1)} %fusion.18), calls=%async_computation.3 | async-start | bytes 1376256 | tf_op jit(solution)/shard_map/all_to_all | solution.py:69
  151.3 21.5 %reduce-scatter.11.cloned.1.call-done = f32[48,1,1024]{2,0,1:T(8,128)} async-done(((f32[48,8,1024]{2,0,1:T(8,128)}), f32[48,1,1024]{2,0,1:T(8,128)}) %reduce-scatter.11.cloned.1.call-update) | async-done | bytes 196624 | tf_op jit(solution)/shard_map/reduce_scatter | solution.py:61
  172.8 36.4 %reduce-scatter.13.cloned.1.call-done = f32[48,1,1024]{2,0,1:T(8,128)} async-done(((f32[48,8,1024]{2,0,1:T(8,128)}), f32[48,1,1024]{2,0,1:T(8,128)}) %reduce-scatter.13.cloned.1.call-update) | async-done | bytes 196624 | tf_op jit(solution)/shard_map/reduce_scatter | solution.py:62
  209.2 1.1 multiply_convert_fusion
  210.3 19.8 %all-gather.1 = bf16[384,1,1024]{2,0,1:T(8,128)(2,1)S(1)} all-gather(bf16[48,1,1024]{2,0,1:T(8,128)(2,1)S(1)} %multiply_convert_fusion), channel_id=3, replica_groups=mesh['dp'=8,'expert'=32] {'dp'}, dimensions={0}, use_global_device_ids=true | all-gather | bytes 884736 | tf_op jit(solution)/shard_map/all_gather | solution.py:67
  230.1 3.3 fusion.21
  233.4 6.6 %all-to-all-start.3 = ((bf16[8,48,896]{2,1,0:T(8,128)(2,1)}), bf16[8,48,896]{2,1,0:T(8,128)(2,1)S(1)}, u32[]{:S(2)}, u32[]{:S(2)}) async-start(bf16[8,48,896]{2,1,0:T(8,128)(2,1)} %fusion.21), calls=%async_computation.7 | async-start | bytes 1376256 | tf_op jit(solution)/shard_map/all_to_all | solution.py:69
  240.0 0.6 dynamic-slice
  241.3 2.5 fusion.1
  243.8 11.5 %all-to-all-done.3 = bf16[8,48,896]{2,1,0:T(8,128)(2,1)S(1)} async-done(((bf16[8,48,896]{2,1,0:T(8,128)(2,1)}), bf16[8,48,896]{2,1,0:T(8,128)(2,1)S(1)}, u32[]{:S(2)}, u32[]{:S(2)}) %all-to-all-start.3) | async-done | bytes 688160 | tf_op jit(solution)/shard_map/all_to_all | solution.py:69
  255.4 2.5 fusion
  257.9 361.0 %all-reduce.4 = (bf16[1,128,7168]{2,1,0:T(8,128)(2,1)}, bf16[1,128,7168]{2,1,0:T(8,128)(2,1)}) all-reduce(f32[1,128,7168]{2,1,0:T(8,128)} %fusion, f32[1,128,7168]{2,1,0:T(8,128)} %fusion.1), channel_id=9, replica_groups=mesh['dp'=8,'expert'=32] {'expert'}, use_global_device_ids=true, to_apply=%region_13.14.clone | all-reduce | flops 1835008 | bytes 11010048
  618.9 1.0 dynamic-slice_convert_fusion
  619.9 0.7 pad_maximum_fusion
  (31 shorter events, 1.0 us)
Async XLA Ops:
  6.5 27.7 %copy-start = (bf16[1,896,1024]{2,1,0:T(8,128)(2,1)S(1)}, bf16[1,896,1024]{2,1,0:T(8,128)(2,1)}, u32[]{:S(2)}) copy-start(bf16[1,896,1024]{2,1,0:T(8,128)(2,1)} %param.11) | copy-start | bytes 5505028
  6.5 78.4 %reduce-scatter.7.cloned.1.call-start = ((), (), s32[]{:S(2)}) async-start(), calls=%async_computation.8 | async-start | bytes 1769472 | tf_op jit(solution)/shard_map/reduce_scatter | solution.py:61
  36.4 3.8 copy-start.1
  36.4 3.8 copy-start.2
  36.4 84.0 %reduce-scatter.9.cloned.1.call-start = ((), (), s32[]{:S(2)}) async-start(), calls=%async_computation.9 | async-start | bytes 1769472 | tf_op jit(solution)/shard_map/reduce_scatter | solution.py:62
  40.1 132.7 %reduce-scatter.11.cloned.1.call-start = ((), (), s32[]{:S(2)}) async-start(), calls=%async_computation.10 | async-start | bytes 1769472 | tf_op jit(solution)/shard_map/reduce_scatter | solution.py:61
  74.3 134.9 %reduce-scatter.13.cloned.1.call-start = ((), (), s32[]{:S(2)}) async-start(), calls=%async_computation.11 | async-start | bytes 1769472 | tf_op jit(solution)/shard_map/reduce_scatter | solution.py:62
  144.7 88.7 %all-to-all-start.1 = ((bf16[8,48,896]{2,1,0:T(8,128)(2,1)}), bf16[8,48,896]{2,1,0:T(8,128)(2,1)S(1)}, u32[]{:S(2)}, u32[]{:S(2)}) async-start(bf16[8,48,896]{2,1,0:T(8,128)(2,1)} %fusion.18), calls=%async_computation.3 | async-start | bytes 1376256 | tf_op jit(solution)/shard_map/all_to_all | solution.py:69
  230.1 9.9 %copy-start.3 = (u32[256]{0:T(256)S(1)}, u32[256]{0:T(256)}, u32[]{:S(2)}) copy-start(u32[256]{0:T(256)} %constant.30) | copy-start | bytes 3076
  233.4 21.9 %all-to-all-start.3 = ((bf16[8,48,896]{2,1,0:T(8,128)(2,1)}), bf16[8,48,896]{2,1,0:T(8,128)(2,1)S(1)}, u32[]{:S(2)}, u32[]{:S(2)}) async-start(bf16[8,48,896]{2,1,0:T(8,128)(2,1)} %fusion.21), calls=%async_computation.7 | async-start | bytes 1376256 | tf_op jit(solution)/shard_map/all_to_all | solution.py:69
Sparse Core Ops, SparseCore 0:
  36.5 48.4 reduce-scatter.6
  87.5 32.7 reduce-scatter.8
  122.9 49.8 reduce-scatter.10
  175.2 33.9 reduce-scatter.12
where the time goes:
time: 635 us; the launch traced here: 627 us
  blocking collectives  452 us (71%)
  waiting for transfers between devices  112 us (18%)
  matrix products  27 us (4%)
  between operations  13.9 us (2%)
  starting transfers between devices  13.3 us (2%)
    unnamed x1, blocking collectives  361 us
    reduce_scatter x2, waiting for transfers between devices, expert_outputs(): lax.psum_scatter(up_part, 'dp', scatter_dimension=1, tiled=True)  71.8 us
    all_to_all x2, blocking collectives, expert_outputs(): lax.all_to_all(pieces, 'dp', split_axis=1, concat_axis=1, tiled=True)  51.5 us
    all_gather x2, blocking collectives, expert_outputs(): produced = project_out(lax.all_gather(hidden, 'dp', axis=0, tiled=True))  39.7 us
    reduce_scatter x2, waiting for transfers between devices, expert_outputs(): lax.psum_scatter(gate_part, 'dp', scatter_dimension=1, tiled=True)  28.5 us
    all_to_all x2, starting transfers between devices, expert_outputs(): lax.all_to_all(produced.astype(jnp.bfloat16), 'dp', split_axis=0, concat_...  13.2 us
  transfers between devices with their start and end apart: 6, of which 5 were waited for; matrix products, arithmetic and copies ran while one was open for 4% of the time, Pallas kernels for 0%

commit v1 on v0

v1 whole, which is shorter than its diff:
```python
import jax
import jax.numpy as jnp
from jax import lax
from jax.experimental import pallas as pl
from jax.experimental.pallas import tpu as pltpu
from jax.sharding import PartitionSpec as P

ROUTE_SCALE = 2.5
MESH = pl.DeviceIdType.MESH
F32 = jnp.float32
BF16 = jnp.bfloat16

MB = 2
ROWS = 128
CAP = 48
D = 7168
W = 896
H = 1024
HH = 512
NDP = 8
CH = 4


def div(a, b):
    return lax.div(a, jnp.int32(b))


def rem(a, b):
    return lax.rem(a, jnp.int32(b))


def kernel(
    tok_hbm, scores_ref, ids_ref, slot_ref, wg_hbm, wu_hbm, wd_hbm, out_ref,
    tok, wgu, wd, pick, pk, xin, part, bsend, brecv, hid, yv, zf, e1s, e1r, tf, e2s, e2r, uv,
    fs, fr, rts, rtr,
    s_loc, s_w, r_w, s_rt, r_rt, s_a, r_a, s_f, r_f, s_o, r_o,
    s_b, r_b, s_c, r_c, s_p, r_p, s_e1, r_e1, s_e2, r_e2, s_x, r_x,
):
    dp = lax.axis_index("dp")
    ex = lax.axis_index("expert")
    zl, c = div(dp, 2), rem(dp, 2)
    y, zh, x = div(ex, 8), rem(div(ex, 4), 2), rem(ex, 4)
    z = zh * 4 + zl
    oc = 1 - c
    peer = (zl * 2 + oc, ex)

    def column(zz, cc):
        return (rem(zz, 4) * 2 + cc, (y * 2 + div(zz, 4)) * 4 + x)

    def xdev(xx):
        return (dp, (y * 2 + zh) * 4 + xx)

    def ydev(yy):
        return (dp, (yy * 2 + zh) * 4 + x)

    def remote(src, dst, ssem, rsem, dev):
        return pltpu.make_async_remote_copy(
            src_ref=src, dst_ref=dst, send_sem=ssem, recv_sem=rsem,
            device_id=dev, device_id_type=MESH,
        )

    bar = pltpu.get_barrier_semaphore()
    for a in range(NDP):
        for b in range(2):
            if a or b:
                dev = (rem(dp + a, NDP), (y * 2 + rem(zh + b, 2)) * 4 + x)
                pl.semaphore_signal(bar, inc=1, device_id=dev, device_id_type=MESH)
    for a in range(1, 4):
        pl.semaphore_signal(bar, inc=1, device_id=xdev(rem(x + a, 4)), device_id_type=MESH)
        pl.semaphore_signal(bar, inc=1, device_id=ydev(rem(y + a, 4)), device_id_type=MESH)

    mine = pl.ds(pl.multiple_of(c * HH, 128), HH)
    theirs = pl.ds(pl.multiple_of(oc * HH, 128), HH)
    loads = [
        pltpu.make_async_copy(tok_hbm.at[0], tok.at[0], s_loc.at[0]),
        pltpu.make_async_copy(tok_hbm.at[1], tok.at[1], s_loc.at[1]),
        pltpu.make_async_copy(wg_hbm.at[0, :, mine], wgu.at[c, :, pl.ds(0, HH)], s_loc.at[2]),
        pltpu.make_async_copy(wu_hbm.at[0, :, mine], wgu.at[c, :, pl.ds(HH, HH)], s_loc.at[3]),
        pltpu.make_async_copy(wd_hbm.at[0], wd, s_loc.at[4]),
    ]
    for cp in loads:
        cp.start()

    lane = lax.broadcasted_iota(jnp.int32, (ROWS, 128), 1)
    sub = lax.broadcasted_iota(jnp.int32, (ROWS, 128), 0)
    cols = jnp.zeros((ROWS, 128), F32)
    for mb in range(MB):
        sc = scores_ref[mb]
        ids = ids_ref[mb]
        wts = ROUTE_SCALE * sc / jnp.sum(sc, axis=1, keepdims=True)
        for zz in range(2):
            logical = slot_ref[(y * 2 + zz) * 4 + x]
            hit = ids == logical
            share = jnp.sum(jnp.where(hit, wts, 0.0), axis=1, keepdims=True)
            there = jnp.sum(jnp.where(hit, 1.0, 0.0), axis=1, keepdims=True)
            cols = cols + jnp.where(lane == zz * 4 + mb, there, 0.0)
            cols = cols + jnp.where(lane == zz * 4 + 2 + mb, share, 0.0)
    rows = jnp.transpose(cols)[0:8]
    before = jnp.where(sub < lane, 1.0, 0.0).astype(BF16)
    ranks = jnp.dot(rows.astype(BF16), before, preferred_element_type=F32)
    ranks = jnp.where(rows > 0.0, ranks, -1.0)
    row8 = lax.broadcasted_iota(jnp.int32, (8, 128), 0)
    info = jnp.where(rem(row8, 4) < 2, ranks, rows)
    place = lax.broadcasted_iota(jnp.int32, (CAP, 128), 0).astype(F32)
    for zz in range(2):
        for mb in range(MB):
            r = zz * 4 + mb
            pick[zz, mb] = jnp.where(place == ranks[r : r + 1], 1.0, 0.0).astype(BF16)
    hi, mid = div(lane, 32), rem(div(lane, 8), 4)
    xx = jnp.where(dp < 4, hi, mid)
    yy = jnp.where(dp < 4, mid, hi)
    home = yy * 32 + rem(div(lane, 4), 2) * 16 + xx * 4 + rem(lane, 4)
    order = jnp.where(sub == home, 1.0, 0.0)
    info = jnp.dot(info, order, preferred_element_type=F32, precision=lax.Precision.HIGHEST)
    rts[...] = info
    rtr[dp] = info

    two = jnp.where(c == 1, z + 2, z + 6)
    dest_z = [rem(two, 8)] * 2 + [rem(z + 1, 8)] * 2 + [rem(z + 7, 8)] * 2
    from_z = [rem(zl + 2, 4)] * 2 + [rem(zl + 1, 4)] * 2 + [rem(zl + 3, 4)] * 2
    source = [from_z[n] * 2 + n % 2 for n in range(6)]

    def pack(mb, zz, j):
        piece = tok[mb, :, pl.ds(pl.multiple_of(j * W, 128), W)]
        return jnp.dot(pick[zz, mb], piece, preferred_element_type=F32).astype(BF16)

    def piece_copy(mb, n):
        return remote(
            pk.at[mb, n], xin.at[mb, n % 2, dp], s_a.at[mb, n], r_a.at[mb, dp],
            column(dest_z[n], n % 2),
        )

    def forward_copy(mb, n):
        i = source[n]
        return remote(xin.at[mb, c, i], xin.at[mb, c, i], s_f.at[mb, n], r_f.at[mb, i], peer)

    def own_copy(mb):
        return remote(xin.at[mb, :, dp], xin.at[mb, :, dp], s_o.at[mb], r_o.at[mb], peer)

    def weight_copies():
        return [
            remote(
                wg_hbm.at[0, :, theirs], wgu.at[c, :, pl.ds(0, HH)], s_w.at[0], r_w.at[0], peer
            ),
            remote(
                wu_hbm.at[0, :, theirs], wgu.at[c, :, pl.ds(HH, HH)], s_w.at[1], r_w.at[1], peer
            ),
        ]

    def info_copies():
        out = [
            remote(rts, rtr.at[dp], s_rt.at[n], r_rt.at[dp], column(dest_z[n], n % 2))
            for n in range(6)
        ]
        return out + [remote(rts, rtr.at[dp], s_rt.at[6], r_rt.at[dp], peer)]

    def dispatch(mb):
        for n in range(6):
            pk[mb, n] = pack(mb, div(dest_z[n], 4), rem(dest_z[n], 4) * 2 + n % 2)
            if mb == 0 and n == 0:
                pl.semaphore_wait(bar, 21)
            piece_copy(mb, n).start()
        for k in range(2):
            xin[mb, k, dp] = pack(mb, zh, zl * 2 + k)
        own_copy(mb).start()

    def collect(mb):
        for n in (2, 3, 4, 5, 0, 1):
            i = source[n]
            remote(
                pk.at[mb, n], xin.at[mb, c, i], s_a.at[mb, n], r_a.at[mb, i], peer
            ).wait_recv()
            forward_copy(mb, n).start()
        own = remote(
            xin.at[mb, :, dp], xin.at[mb, :, zl * 2 + oc], s_o.at[mb], r_o.at[mb], peer
        )
        own.wait_recv()
        for n in (2, 3, 4, 5, 0, 1):
            i = source[n]
            remote(
                xin.at[mb, c, i], xin.at[mb, oc, i], s_f.at[mb, n], r_f.at[mb, i], peer
            ).wait_recv()

    def project_in(mb):
        @pl.loop(0, 4)
        def _(nb):
            at = pl.ds(pl.multiple_of(nb * 256, 128), 256)
            total = jnp.dot(
                xin[mb, 0].reshape(NDP * CAP, W), wgu[0, :, at], preferred_element_type=F32
            ) + jnp.dot(
                xin[mb, 1].reshape(NDP * CAP, W), wgu[1, :, at], preferred_element_type=F32
            )
            part[mb, :, :, at] = total.reshape(NDP, CAP, 256)

    def chain(d, k):
        mb, i = div(k, CH), rem(k, CH) + 4 * (1 - d)
        p = zl if d == 0 else 3 - zl
        up = (dp + 2 if d == 0 else dp - 2, ex)
        down = (dp - 2 if d == 0 else dp + 2, ex)
        slot = hid.at[mb, c, i]
        sums = remote(bsend.at[d, k], brecv.at[d, k], s_b.at[d, k], r_b.at[d, k], up)
        relay = remote(slot, slot, s_c.at[d, k], r_c.at[d, k], down)
        across = remote(slot, slot, s_p.at[d, k], r_p.at[d, k], peer)
        return mb, i, p, sums, relay, across

    def chain_step(t):
        for d in range(2):
            p0 = zl if d == 0 else 3 - zl
            k = t - p0

            @pl.when((k >= 0) & (k < MB * CH))
            def _():
                mb, i, p, sums, relay, across = chain(d, k)

                @pl.when(p == 0)
                def _():
                    bsend[d, k] = part[mb, i].astype(BF16)

                @pl.when(p > 0)
                def _():
                    sums.wait_recv()

                @pl.when((p > 0) & (p < 3))
                def _():
                    bsend[d, k] = (part[mb, i] + brecv[d, k].astype(F32)).astype(BF16)

                @pl.when(p < 3)
                def _():
                    sums.start()

                @pl.when(p == 3)
                def _():
                    gate = part[mb, i, :, 0:HH] + brecv[d, k, :, 0:HH].astype(F32)
                    lift = part[mb, i, :, HH:H] + brecv[d, k, :, HH:H].astype(F32)
                    hid[mb, c, i] = (gate / (1.0 + jnp.exp(-gate)) * lift).astype(BF16)
                    relay.start()
                    across.start()

            k2 = t - 6 + p0

            @pl.when((p0 < 3) & (k2 >= 0) & (k2 < MB * CH))
            def _():
                mb, i, p, sums, relay, across = chain(d, k2)
                relay.wait_recv()

                @pl.when(p > 0)
                def _():
                    relay.start()

                across.start()

    def chain_sends():
        @pl.loop(0, MB * CH)
        def _(k):
            for d in range(2):
                mb, i, p, sums, relay, across = chain(d, k)

                @pl.when(p < 3)
                def _():
                    sums.wait_send()

                @pl.when(p > 0)
                def _():
                    relay.wait_send()

                across.wait_send()

    def project_out(mb):
        for d in range(2):
            for q in range(CH):
                i = q + 4 * (1 - d)
                remote(
                    hid.at[mb, c, i], hid.at[mb, oc, i],
                    s_p.at[d, mb * CH + q], r_p.at[d, mb * CH + q], peer,
                ).wait_recv()
        rows_out = jnp.dot(
            hid[mb, 0].reshape(NDP * CAP, HH), wd[0:HH], preferred_element_type=F32
        ) + jnp.dot(hid[mb, 1].reshape(NDP * CAP, HH), wd[HH:H], preferred_element_type=F32)
        yv[...] = rows_out.astype(BF16).reshape(NDP, CAP, W)

    def e1_copy(mb, g, a):
        to = rem((x if g == 0 else y) + a, 4)
        dev = xdev(to) if g == 0 else ydev(to)
        return remote(
            e1s.at[mb, g, to], e1r.at[mb, g, a - 1], s_e1.at[mb, g, a - 1],
            r_e1.at[mb, g, a - 1], dev,
        )

    def e2_copy(mb, g, a):
        to = rem((y if g == 0 else x) + a, 4)
        dev = ydev(to) if g == 0 else xdev(to)
        return remote(
            e2s.at[mb, g, to], e2r.at[mb, g, a - 1], s_e2.at[mb, g, a - 1],
            r_e2.at[mb, g, a - 1], dev,
        )

    def spread(mb):
        spot = lax.broadcasted_iota(jnp.int32, (ROWS, CAP), 1).astype(F32)
        for g in range(2):
            for ii in range(4):
                turned = jnp.transpose(rtr[g * 4 + ii])
                rank = jnp.where(zh == 0, turned[:, mb : mb + 1], turned[:, 4 + mb : 5 + mb])
                share = jnp.where(
                    zh == 0, turned[:, 2 + mb : 3 + mb], turned[:, 6 + mb : 7 + mb]
                )
                one = jnp.where(rank == spot, 1.0, 0.0).astype(BF16)
                value = share * jnp.dot(one, yv[g * 4 + ii], preferred_element_type=F32)
                value = value.reshape(4, 32, W)
                zf[g, :, ii] = value
                e1s[mb, g, :, ii] = value.astype(BF16)
            for a in (2, 1, 3):
                e1_copy(mb, g, a).start()

    def combine1(mb):
        for g in range(2):
            for a in (1, 3, 2):
                e1_copy(mb, g, a).wait_recv()
            own = x if g == 0 else y
            for ii in range(4):
                total = zf[g, own, ii]
                for a in range(3):
                    total = total + e1r[mb, g, a, ii].astype(F32)
                tf[g, :, ii] = total.reshape(4, 8, W)
            for b in range(4):
                e2s[mb, g, b] = tf[g, b].reshape(32, W).astype(BF16)
            for a in (2, 1, 3):
                e2_copy(mb, g, a).start()

    def combine2(mb):
        for g in range(2):
            for a in (1, 3, 2):
                e2_copy(mb, g, a).wait_recv()
            own = y if g == 0 else x
            total = tf[g, own].reshape(32, W)
            for a in range(3):
                total = total + e2r[mb, g, a].astype(F32)
            uv[mb, g] = total.reshape(4, 8, W)

    def deliver_copy(a, b):
        i, zz = rem(dp + a, NDP), rem(zh + b, 2)
        dev = (i, (y * 2 + zz) * 4 + x)
        n = a * 2 + b
        return remote(fs.at[n], fr.at[dp, zh], s_x.at[n], r_x.at[dp, zh], dev)

    def deliver():
        top = lax.broadcasted_iota(jnp.int32, (8, W), 0) < 4
        for a in (4, 3, 5, 2, 6, 1, 7, 0):
            i = rem(dp + a, NDP)
            u0, u1 = uv[0, div(i, 4), rem(i, 4)], uv[1, div(i, 4), rem(i, 4)]
            first = jnp.where(top, u0, pltpu.roll(u1, 4, 0))
            second = jnp.where(top, pltpu.roll(u0, 4, 0), u1)
            same = jnp.where(zh == 0, first, second)
            other = jnp.where(zh == 0, second, first)
            fs[a * 2 + 1] = other
            deliver_copy(a, 1).start()
            if a:
                fs[a * 2] = same
                deliver_copy(a, 0).start()
            else:
                fr[dp, zh] = same
        for a in range(NDP):
            for b in range(2):
                if a or b:
                    j, zz = rem(dp + NDP - a, NDP), rem(zh + b, 2)
                    remote(
                        fs.at[a * 2 + b], fr.at[j, zz], s_x.at[a * 2 + b], r_x.at[j, zz], peer
                    ).wait_recv()
        for j in range(NDP):
            out_ref[:, j * W : (j + 1) * W] = (fr[j, 0] + fr[j, 1]).astype(BF16)

    loads[0].wait()
    dispatch(0)
    for cp in weight_copies():
        cp.start()
    for cp in info_copies():
        cp.start()
    loads[1].wait()
    dispatch(1)
    loads[2].wait()
    loads[3].wait()
    for k in range(2):
        at = pl.ds(k * HH, HH)
        remote(
            wg_hbm.at[0, :, theirs], wgu.at[oc, :, at], s_w.at[k], r_w.at[k], peer
        ).wait_recv()
    collect(0)
    project_in(0)

    @pl.loop(0, CH)
    def _(t):
        chain_step(t)

    collect(1)
    project_in(1)

    @pl.loop(CH, CH + 6)
    def _(t):
        chain_step(t)

    loads[4].wait()
    for n in range(6):
        remote(rts, rtr.at[source[n]], s_rt.at[n], r_rt.at[source[n]], peer).wait_recv()
    remote(rts, rtr.at[zl * 2 + oc], s_rt.at[6], r_rt.at[zl * 2 + oc], peer).wait_recv()
    project_out(0)
    spread(0)

    @pl.loop(CH + 6, 2 * CH + 6)
    def _(t):
        chain_step(t)

    combine1(0)
    project_out(1)
    spread(1)
    combine2(0)
    combine1(1)
    combine2(1)
    deliver()

    for cp in weight_copies() + info_copies():
        cp.wait_send()
    chain_sends()
    for mb in range(MB):
        own_copy(mb).wait_send()
        for n in range(6):
            piece_copy(mb, n).wait_send()
            forward_copy(mb, n).wait_send()
        for g in range(2):
            for a in range(1, 4):
                e1_copy(mb, g, a).wait_send()
                e2_copy(mb, g, a).wait_send()
    for a in range(NDP):
        for b in range(2):
            if a or b:
                deliver_copy(a, b).wait_send()


def per_device(tokens, scores, expert_ids, slot_expert, w_gate, w_up, w_down):
    vmem = pl.BlockSpec(memory_space=pltpu.VMEM)
    anywhere = pl.BlockSpec(memory_space=pl.ANY)
    dma = pltpu.SemaphoreType.DMA
    out = pl.pallas_call(
        kernel,
        out_shape=jax.ShapeDtypeStruct((8, D), BF16),
        in_specs=[
            anywhere, vmem, vmem, pl.BlockSpec(memory_space=pltpu.SMEM),
            anywhere, anywhere, anywhere,
        ],
        out_specs=vmem,
        scratch_shapes=[
            pltpu.VMEM((MB, ROWS, D), BF16),
            pltpu.VMEM((2, W, H), BF16),
            pltpu.VMEM((H, W), BF16),
            pltpu.VMEM((2, MB, CAP, 128), BF16),
            pltpu.VMEM((MB, 6, CAP, W), BF16),
            pltpu.VMEM((MB, 2, NDP, CAP, W), BF16),
            pltpu.VMEM((MB, NDP, CAP, H), F32),
            pltpu.VMEM((2, MB * CH, CAP, H), BF16),
            pltpu.VMEM((2, MB * CH, CAP, H), BF16),
            pltpu.VMEM((MB, 2, NDP, CAP, HH), BF16),
            pltpu.VMEM((NDP, CAP, W), BF16),
            pltpu.VMEM((2, 4, 4, 32, W), F32),
            pltpu.VMEM((MB, 2, 4, 4, 32, W), BF16),
            pltpu.VMEM((MB, 2, 3, 4, 32, W), BF16),
            pltpu.VMEM((2, 4, 4, 8, W), F32),
            pltpu.VMEM((MB, 2, 4, 32, W), BF16),
            pltpu.VMEM((MB, 2, 3, 32, W), BF16),
            pltpu.VMEM((MB, 2, 4, 8, W), F32),
            pltpu.VMEM((16, 8, W), F32),
            pltpu.VMEM((NDP, 2, 8, W), F32),
            pltpu.VMEM((8, 128), F32),
            pltpu.VMEM((NDP, 8, 128), F32),
            dma((5,)),
            dma((2,)), dma((2,)),
            dma((7,)), dma((NDP,)),
            dma((MB, 6)), dma((MB, NDP)),
            dma((MB, 6)), dma((MB, NDP)),
            dma((MB,)), dma((MB,)),
            dma((2, MB * CH)), dma((2, MB * CH)),
            dma((2, MB * CH)), dma((2, MB * CH)),
            dma((2, MB * CH)), dma((2, MB * CH)),
            dma((MB, 2, 3)), dma((MB, 2, 3)),
            dma((MB, 2, 3)), dma((MB, 2, 3)),
            dma((16,)), dma((NDP, 2)),
        ],
        compiler_params=pltpu.CompilerParams(
            collective_id=0, has_side_effects=True, vmem_limit_bytes=56 * 2**20
        ),
        name="expert_layer",
    )(tokens, scores, expert_ids, slot_expert, w_gate, w_up, w_down)
    return out.reshape(MB, 4, D)


def solution(mesh):
    in_specs = (
        P(None, "dp", None),
        P(None, "dp", None),
        P(None, "dp", None),
        P(),
        P("expert", "dp", None),
        P("expert", "dp", None),
        P("expert", None, "dp"),
    )
    out_specs = P(None, ("dp", "expert"), None)
    return jax.shard_map(
        per_device, mesh=mesh, in_specs=in_specs, out_specs=out_specs, check_vma=False
    )
```

time: 635 us -> 115 us (0.18)
  blocking collectives: 452 us -> 0 us
  waiting for transfers between devices: 112 us -> 0 us
  Pallas kernels: 0 us -> 109 us
  matrix products: 27 us -> 0 us
  between operations: 13.9 us -> 0.01 us
  starting transfers between devices: 13.3 us -> 0 us
    unnamed x1 -> x0, blocking collectives: 361 us -> none
    pallas_call x0 -> x1, Pallas kernels: none -> 109 us  [per_device(): pl.pallas_call(kernel, out_shape=jax.ShapeDtypeStruct((8, D), BF16), in_s...]
    reduce_scatter x4 -> x0, waiting for transfers between devices: 100 us -> none  [the longest x2 71.8 us: expert_outputs(): lax.psum_scatter(up_part, 'dp', scatter_dimension=1, tiled=True)]
    all_to_all x2 -> x0, blocking collectives: 51.5 us -> none  [expert_outputs(): lax.all_to_all(pieces, 'dp', split_axis=1, concat_axis=1, tiled=True)]
    all_gather x2 -> x0, blocking collectives: 39.7 us -> none  [expert_outputs(): produced = project_out(lax.all_gather(hidden, 'dp', axis=0, tiled=True))]
    dot_general x10 -> x0, matrix products: 27 us -> none  [the longest x2 7.3 us: project_in(): jnp.einsum('rsd,dh->rsh', received, up_local, preferred_element_type=jnp....]
    all_to_all x2 -> x0, starting transfers between devices: 13.2 us -> none  [expert_outputs(): lax.all_to_all(produced.astype(jnp.bfloat16), 'dp', split_axis=0, concat_...]
    all_to_all x2 -> x0, waiting for transfers between devices: 11.5 us -> none  [expert_outputs(): lax.all_to_all(produced.astype(jnp.bfloat16), 'dp', split_axis=0, concat_...]
  transfers between devices with their start and end apart: 6 -> 0, of which waited for: 5 -> 0; matrix products, arithmetic and copies ran while one was open for 4% -> 0% of each run, Pallas kernels for 0% -> 0%
where the time goes in v1:
time: 115 us; the launch traced here: 113 us
  Pallas kernels  109 us (95%)
  local copies, waits for them, and re-layouts  4.54 us (4%)
    pallas_call x1, Pallas kernels, per_device(): pl.pallas_call(kernel, out_shape=jax.ShapeDtypeStruct((8, D), BF16), in_s...  109 us
    unnamed x2, local copies, waits for them, and re-layouts  2.95 us

profile of v1, /device:TPU:33, one launch (start us, length us, event | category | flops | bytes accessed | tf_op | source)
XLA Modules:
  0.0 113.1 jit_solution(8074038894810436501)
XLA Ops:
  0.0 1.5 %copy.8.scores_ref = f32[2,128,8]{2,1,0:T(8,128)} copy(f32[2,128,8]{1,2,0:T(8,128)} %param.8) | data formatting | bytes 16384 | tf_op args[1]
  1.5 1.5 %copy.9.ids_ref = s32[2,128,8]{2,1,0:T(8,128)} copy(s32[2,128,8]{1,2,0:T(8,128)} %param.9) | data formatting | bytes 16384 | tf_op args[2]
  2.9 108.5 %expert_layer.1 = bf16[8,7168]{1,0:T(8,128)(2,1)} custom-call(bf16[2,128,7168]{2,1,0:T(8,128)(2,1)} %tok_hbm.1, f32[2,128,8]{2,1,0:T(8,128)} %copy.8.scores_ref, s32[2,128,8]{2,1,0:T(8,128)} %copy.9.ids_ref, s32[32]{0:T(128)} %slot_ref.1, bf16[1,896,1024]{2,1,0:T(8,128)(2,1)} %wg_hbm.1, bf16[1,896,1024]{2,1,0:T(8,128)(2,1)} %wu_hbm.1, ...), custom_call_target="tpu_custom_call" | custom-call | tf_op jit(solution)/shard_map/expert_layer/pallas_call | solution.py:441
  111.5 1.6 %reshape.3 = bf16[2,4,7168]{2,1,0:T(4,128)(2,1)} reshape(bf16[8,7168]{1,0:T(8,128)(2,1)} %expert_layer.1) | data formatting | bytes 229376 | tf_op jit(solution)/shard_map/reshape | solution.py:490

commit v2 on v1

v2 whole, which is shorter than its diff:
```python
import jax
import jax.numpy as jnp
from jax import lax
from jax.experimental import pallas as pl
from jax.experimental.pallas import tpu as pltpu
from jax.sharding import PartitionSpec as P

ROUTE_SCALE = 2.5
MESH = pl.DeviceIdType.MESH
F32 = jnp.float32
BF16 = jnp.bfloat16

MB = 2
ROWS = 128
CAP = 48
D = 7168
W = 896
H = 1024
HH = 512
NDP = 8
HQ = 256
NCH = 16
UNITS = 8
WF = 512
SKEW = 3
PIECES = 16
LAG0 = 6 * SKEW + 2
LAG1 = LAG0 + 6
LAG2 = LAG1 + 6
LAG3 = LAG2 + 6


def div(a, b):
    return lax.div(a, jnp.int32(b))


def rem(a, b):
    return lax.rem(a, jnp.int32(b))


def kernel(
    tok_hbm, scores_ref, ids_ref, slot_ref, wg_hbm, wu_hbm, wd_hbm, out_ref,
    tok, wgu, wd, pick, pk, xin, part, bsend, brecv, hid, zf, zown, keep, e1s, e1r, m1s, m1r, e2s, e2r,
    fs, fr, rts, rtr,
    s_loc, s_w, r_w, s_rt, r_rt, s_a, r_a, s_f, r_f, s_o, r_o,
    s_b, r_b, s_c, r_c, s_p, r_p, s_e1, r_e1, s_m1, r_m1, s_e2, r_e2, s_x, r_x,
):
    dp = lax.axis_index("dp")
    ex = lax.axis_index("expert")
    zl, c = div(dp, 2), rem(dp, 2)
    y, zh, x = div(ex, 8), rem(div(ex, 4), 2), rem(ex, 4)
    z = zh * 4 + zl
    oc = 1 - c
    peer = (zl * 2 + oc, ex)

    def column(zz, cc):
        return (rem(zz, 4) * 2 + cc, (y * 2 + div(zz, 4)) * 4 + x)

    def xdev(xx):
        return (dp, (y * 2 + zh) * 4 + xx)

    def ydev(yy):
        return (dp, (yy * 2 + zh) * 4 + x)

    def remote(src, dst, ssem, rsem, dev):
        return pltpu.make_async_remote_copy(
            src_ref=src, dst_ref=dst, send_sem=ssem, recv_sem=rsem,
            device_id=dev, device_id_type=MESH,
        )

    bar = pltpu.get_barrier_semaphore()
    for a in range(NDP):
        for b in range(2):
            if a or b:
                dev = (rem(dp + a, NDP), (y * 2 + rem(zh + b, 2)) * 4 + x)
                pl.semaphore_signal(bar, inc=1, device_id=dev, device_id_type=MESH)
    for a in range(1, 4):
        pl.semaphore_signal(bar, inc=1, device_id=xdev(rem(x + a, 4)), device_id_type=MESH)
        pl.semaphore_signal(bar, inc=1, device_id=ydev(rem(y + a, 4)), device_id_type=MESH)

    def hidden_at(core, half):
        return pl.ds(pl.multiple_of(core * HH + half * HQ, 128), HQ)

    def weight_at(k):
        return (wg_hbm, wu_hbm)[k % 2], pl.ds(k * HQ, HQ)

    loads = [pltpu.make_async_copy(tok_hbm.at[mb], tok.at[mb], s_loc.at[mb]) for mb in range(MB)]
    for k in range(4):
        ref, at = weight_at(k)
        loads.append(
            pltpu.make_async_copy(
                ref.at[0, :, hidden_at(c, k // 2)], wgu.at[c, :, at], s_loc.at[2 + k]
            )
        )
    loads.append(pltpu.make_async_copy(wd_hbm.at[0], wd, s_loc.at[6]))
    for cp in loads:
        cp.start()

    row8 = lax.broadcasted_iota(jnp.int32, (8, ROWS), 0)
    rows = jnp.zeros((8, ROWS), F32)
    for mb in range(MB):
        sc = scores_ref[mb]
        ids = ids_ref[mb]
        wts = ROUTE_SCALE * sc / jnp.sum(sc, axis=0, keepdims=True)
        for zz in range(2):
            logical = slot_ref[(y * 2 + zz) * 4 + x]
            hit = ids == logical
            share = jnp.sum(jnp.where(hit, wts, 0.0), axis=0, keepdims=True)
            there = jnp.sum(jnp.where(hit, 1.0, 0.0), axis=0, keepdims=True)
            rows = jnp.where(row8 == zz * 4 + mb, there, rows)
            rows = jnp.where(row8 == zz * 4 + 2 + mb, share, rows)
    lane = lax.broadcasted_iota(jnp.int32, (ROWS, ROWS), 1)
    sub = lax.broadcasted_iota(jnp.int32, (ROWS, ROWS), 0)
    before = jnp.where(sub < lane, 1.0, 0.0).astype(BF16)
    ranks = jnp.dot(rows.astype(BF16), before, preferred_element_type=F32)
    ranks = jnp.where(rows > 0.0, ranks, -1.0)
    info = jnp.where(rem(row8, 4) < 2, ranks, rows)
    place = lax.broadcasted_iota(jnp.int32, (CAP, ROWS), 0).astype(F32)
    for zz in range(2):
        for mb in range(MB):
            r = zz * 4 + mb
            pick[zz, mb] = jnp.where(place == ranks[r : r + 1], 1.0, 0.0).astype(BF16)

    two = jnp.where(c == 1, z + 2, z + 6)
    dest_z = [rem(two, 8)] * 2 + [rem(z + 1, 8)] * 2 + [rem(z + 7, 8)] * 2
    from_z = [rem(zl + 2, 4)] * 2 + [rem(zl + 1, 4)] * 2 + [rem(zl + 3, 4)] * 2
    source = [from_z[n] * 2 + n % 2 for n in range(6)]

    def pack(mb, zz, j):
        piece = tok[mb, :, pl.ds(pl.multiple_of(j * W, 128), W)]
        return jnp.dot(pick[zz, mb], piece, preferred_element_type=F32).astype(BF16)

    def piece_copy(mb, n):
        return remote(
            pk.at[mb, n], xin.at[mb, n % 2, dp], s_a.at[mb, n], r_a.at[mb, dp],
            column(dest_z[n], n % 2),
        )

    def forward_copy(mb, n):
        i = source[n]
        return remote(xin.at[mb, c, i], xin.at[mb, c, i], s_f.at[mb, n], r_f.at[mb, i], peer)

    def own_copy(mb):
        return remote(xin.at[mb, :, dp], xin.at[mb, :, dp], s_o.at[mb], r_o.at[mb], peer)

    def weight_copies():
        out = []
        for k in range(4):
            ref, at = weight_at(k)
            out.append(
                remote(
                    ref.at[0, :, hidden_at(oc, k // 2)], wgu.at[c, :, at],
                    s_w.at[k], r_w.at[k], peer,
                )
            )
        return out

    def info_copies():
        out = [
            remote(rts, rtr.at[dp], s_rt.at[n], r_rt.at[dp], column(dest_z[n], n % 2))
            for n in range(6)
        ]
        return out + [remote(rts, rtr.at[dp], s_rt.at[6], r_rt.at[dp], peer)]

    def dispatch(mb):
        for n in range(6):
            pk[mb, n] = pack(mb, div(dest_z[n], 4), rem(dest_z[n], 4) * 2 + n % 2)
            if mb == 0 and n == 0:
                pl.semaphore_wait(bar, 21)
            piece_copy(mb, n).start()
        for k in range(2):
            xin[mb, k, dp] = pack(mb, zh, zl * 2 + k)
        own_copy(mb).start()

    def announce():
        hi, mid = div(lane, 32), rem(div(lane, 8), 4)
        xx = jnp.where(dp < 4, hi, mid)
        yy = jnp.where(dp < 4, mid, hi)
        home = yy * 32 + rem(div(lane, 4), 2) * 16 + xx * 4 + rem(lane, 4)
        order = jnp.where(sub == home, 1.0, 0.0)
        told = jnp.dot(info, order, preferred_element_type=F32, precision=lax.Precision.HIGHEST)
        rts[...] = told
        rtr[dp] = told
        for cp in info_copies():
            cp.start()

    def collect(mb):
        for n in (2, 3, 4, 5, 0, 1):
            i = source[n]
            remote(
                pk.at[mb, n], xin.at[mb, c, i], s_a.at[mb, n], r_a.at[mb, i], peer
            ).wait_recv()
            forward_copy(mb, n).start()
        own = remote(
            xin.at[mb, :, dp], xin.at[mb, :, zl * 2 + oc], s_o.at[mb], r_o.at[mb], peer
        )
        own.wait_recv()
        for n in (2, 3, 4, 5, 0, 1):
            i = source[n]
            remote(
                xin.at[mb, c, i], xin.at[mb, oc, i], s_f.at[mb, n], r_f.at[mb, i], peer
            ).wait_recv()

    def project_in(mb, n):
        at = pl.ds(n * HQ, HQ)
        total = jnp.dot(
            xin[mb, 0].reshape(NDP * CAP, W), wgu[0, :, at], preferred_element_type=F32
        ) + jnp.dot(
            xin[mb, 1].reshape(NDP * CAP, W), wgu[1, :, at], preferred_element_type=F32
        )
        part[mb, :, n // 2, :, (n % 2) * HQ : (n % 2 + 1) * HQ] = total.reshape(NDP, CAP, HQ)

    def chain(d, k):
        half, u = rem(k, 2), div(k, 2)
        q, mb = rem(u, 4), div(u, 4)
        p = zl if d == 0 else 3 - zl
        up = (dp + 2 if d == 0 else dp - 2, ex)
        down = (dp - 2 if d == 0 else dp + 2, ex)
        slot = hid.at[u, c, half, 1 - d]
        own = part.at[mb, q + 4 * (1 - d), half]
        sums = remote(bsend.at[d, k], brecv.at[d, k], s_b.at[d, k], r_b.at[d, k], up)
        relay = remote(slot, slot, s_c.at[d, k], r_c.at[d, k], down)
        across = remote(slot, slot, s_p.at[d, k], r_p.at[d, k], peer)
        return own, slot, p, sums, relay, across

    def chain_step(t):
        for d in range(2):
            p0 = zl if d == 0 else 3 - zl
            k = t - SKEW * p0

            @pl.when((k >= 0) & (k < NCH))
            def _():
                own, slot, p, sums, relay, across = chain(d, k)

                @pl.when(p == 0)
                def _():
                    bsend[d, k] = own[...].astype(BF16)

                @pl.when(p > 0)
                def _():
                    sums.wait_recv()

                @pl.when((p > 0) & (p < 3))
                def _():
                    bsend[d, k] = (own[...] + brecv[d, k].astype(F32)).astype(BF16)

                @pl.when(p < 3)
                def _():
                    sums.start()

                @pl.when(p == 3)
                def _():
                    gate = own[:, 0:HQ] + brecv[d, k, :, 0:HQ].astype(F32)
                    lift = own[:, HQ : 2 * HQ] + brecv[d, k, :, HQ : 2 * HQ].astype(F32)
                    slot[...] = (gate / (1.0 + jnp.exp(-gate)) * lift).astype(BF16)
                    relay.start()
                    across.start()

        for d in range(2):
            p0 = zl if d == 0 else 3 - zl
            k2 = t - SKEW * (6 - p0)

            @pl.when((p0 < 3) & (k2 >= 0) & (k2 < NCH))
            def _():
                own, slot, p, sums, relay, across = chain(d, k2)
                relay.wait_recv()

                @pl.when(p > 0)
                def _():
                    relay.start()

                across.start()

    def chain_sends():
        @pl.loop(0, NCH)
        def _(k):
            for d in range(2):
                own, slot, p, sums, relay, across = chain(d, k)

                @pl.when(p < 3)
                def _():
                    sums.wait_send()

                @pl.when(p > 0)
                def _():
                    relay.wait_send()

                across.wait_send()

    def split(w):
        u, g = div(w, 2), rem(w, 2)
        return u, g, div(u, 4), rem(u, 4)

    def project_out(w):
        u, g, mb, q = split(w)
        for half in range(2):
            there = hid.at[u, oc, half, g]
            k = u * 2 + half
            remote(there, there, s_p.at[1 - g, k], r_p.at[1 - g, k], peer).wait_recv()
        total = jnp.zeros((CAP, W), F32)
        for core in range(2):
            for half in range(2):
                total = total + jnp.dot(
                    hid[u, core, half, g],
                    wd[core * HH + half * HQ : core * HH + (half + 1) * HQ],
                    preferred_element_type=F32,
                )
        return total.astype(BF16)

    def expert_at(g, a, first):
        along_x = (g == 0) == first
        to_x = jnp.where(along_x, rem(x + a, 4), x)
        to_y = jnp.where(along_x, y, rem(y + a, 4))
        return (dp, (to_y * 2 + zh) * 4 + to_x)

    def e1_copy(w, d):
        dev = expert_at(rem(w, 2), 1 if d == 0 else 3, True)
        return remote(e1s.at[w, d], e1r.at[w, d], s_e1.at[w, d], r_e1.at[w, d], dev)

    def m1_copy(w, d):
        dev = expert_at(rem(w, 2), 1 if d == 0 else 3, True)
        return remote(m1s.at[w, d], m1r.at[w, d], s_m1.at[w, d], r_m1.at[w, d], dev)

    def e2_copy(w, a):
        g = rem(w, 2)
        to = rem(jnp.where(g == 0, y, x) + a, 4)
        dev = expert_at(g, a, False)
        return remote(
            e2s.at[w, to], e2r.at[w, a - 1], s_e2.at[w, a - 1], r_e2.at[w, a - 1], dev
        )

    def spread(w):
        u, g, mb, q = split(w)
        rows_out = project_out(w)
        spot = lax.broadcasted_iota(jnp.int32, (ROWS, CAP), 1).astype(F32)
        row = lax.broadcasted_iota(jnp.int32, (8, ROWS), 0)
        told = rtr[g * 4 + q]
        rank = jnp.sum(jnp.where(row == zh * 4 + mb, told, 0.0), axis=0, keepdims=True)
        share = jnp.sum(jnp.where(row == zh * 4 + 2 + mb, told, 0.0), axis=0, keepdims=True)
        turned = jnp.transpose(jnp.where(row == 0, rank, share))
        one = jnp.where(turned[:, 0:1] == spot, 1.0, 0.0).astype(BF16)
        value = turned[:, 1:2] * jnp.dot(one, rows_out, preferred_element_type=F32)
        zf[...] = value.reshape(4, 32, W)
        at = jnp.where(g == 0, x, y)
        above, far, below = rem(at + 1, 4), rem(at + 2, 4), rem(at + 3, 4)
        e1s[w, 0, 0:16] = zf[far, 0:16].astype(BF16)
        e1s[w, 0, 16:32] = zf[above, 16:32].astype(BF16)
        e1s[w, 1, 0:16] = zf[far, 16:32].astype(BF16)
        e1s[w, 1, 16:32] = zf[below, 0:16].astype(BF16)
        for d in range(2):
            e1_copy(w, d).start()
        keep[w, 0] = zf[above, 0:16]
        keep[w, 1] = zf[below, 16:32]
        zown[w] = zf[at]

    def merge(w):
        for d in range(2):
            e1_copy(w, d).wait_recv()
            m1s[w, d] = (keep[w, d] + e1r[w, d, 0:16].astype(F32)).astype(BF16)
            m1_copy(w, d).start()

    def combine1(w):
        for d in range(2):
            m1_copy(w, d).wait_recv()
        for d in range(2):
            rows = slice(16 * d, 16 * d + 16)
            total = zown[w, rows] + e1r[w, 1 - d, 16:32].astype(F32)
            total = total + m1r[w, d].astype(F32)
            e2s[w, 2 * d : 2 * d + 2] = total.reshape(2, 8, W)
        for a in (2, 1, 3):
            e2_copy(w, a).start()

    def deliver_copy(w, zz):
        u, g, mb, q = split(w)
        i = q + 4 * g
        dev = (i, (y * 2 + zz) * 4 + x)
        away = (i != dp) | (zh != zz)
        return away, remote(
            fs.at[w, zz], fr.at[mb, dp, zh], s_x.at[w, zz], r_x.at[mb, dp, zh], dev
        )

    def combine2(w):
        u, g, mb, q = split(w)
        top = lax.broadcasted_iota(jnp.int32, (8, WF), 0) < 4
        for a in (1, 3, 2):
            e2_copy(w, a).wait_recv()
        total = e2s[w, jnp.where(g == 0, y, x)]
        for a in range(3):
            total = total + e2r[w, a]
        lo = total[:, 0:WF]
        hi = jnp.concatenate([total[:, WF:W], jnp.zeros((8, 2 * WF - W), F32)], axis=1)
        fs[w, 0] = jnp.where(top, lo, pltpu.roll(hi, 4, 0))
        fs[w, 1] = jnp.where(top, pltpu.roll(lo, 4, 0), hi)
        for zz in range(2):
            away, cp = deliver_copy(w, zz)

            @pl.when(away)
            def _():
                cp.start()

            @pl.when(jnp.logical_not(away))
            def _():
                fr[mb, dp, zh] = fs[w, zz]

    def finish(mb):
        for a in range(NDP):
            for b in range(2):
                if a or b:
                    j, zz = rem(dp + NDP - a, NDP), rem(zh + b, 2)
                    remote(
                        fs.at[0, 0], fr.at[mb, j, zz], s_x.at[0, 0], r_x.at[mb, j, zz], peer
                    ).wait_recv()
        for j in range(NDP):
            total = (fr[mb, j, 0] + fr[mb, j, 1]).astype(BF16)
            out_ref[mb, :, j * W : j * W + WF] = total[0:4]
            out_ref[mb, :, j * W + WF : (j + 1) * W] = total[4:8, 0 : W - WF]

    loads[0].wait()
    dispatch(0)
    for cp in weight_copies():
        cp.start()
    loads[1].wait()
    dispatch(1)
    announce()
    for k in range(4):
        loads[2 + k].wait()
    for k in range(4):
        ref, at = weight_at(k)
        remote(
            ref.at[0, :, hidden_at(oc, k // 2)], wgu.at[oc, :, at], s_w.at[k], r_w.at[k], peer
        ).wait_recv()
    collect(0)
    for n in range(4):
        project_in(0, n)

    @pl.loop(0, 4)
    def _(t):
        chain_step(t)

    collect(1)
    for n in range(4):
        chain_step(4 + n)
        project_in(1, n)
    loads[6].wait()
    for n in range(6):
        remote(rts, rtr.at[source[n]], s_rt.at[n], r_rt.at[source[n]], peer).wait_recv()
    remote(rts, rtr.at[zl * 2 + oc], s_rt.at[6], r_rt.at[zl * 2 + oc], peer).wait_recv()

    @pl.loop(8, PIECES + LAG3)
    def _(t):
        chain_step(t)

        @pl.when(t >= LAG3)
        def _():
            combine2(t - LAG3)

        @pl.when((t >= LAG2) & (t < LAG2 + PIECES))
        def _():
            combine1(t - LAG2)

        @pl.when((t >= LAG1) & (t < LAG1 + PIECES))
        def _():
            merge(t - LAG1)

        @pl.when((t >= LAG0) & (t < LAG0 + PIECES))
        def _():
            spread(t - LAG0)

    finish(0)
    finish(1)

    for cp in weight_copies() + info_copies():
        cp.wait_send()
    chain_sends()
    for mb in range(MB):
        own_copy(mb).wait_send()
        for n in range(6):
            piece_copy(mb, n).wait_send()
            forward_copy(mb, n).wait_send()

    @pl.loop(0, PIECES)
    def _(w):
        for d in range(2):
            e1_copy(w, d).wait_send()
            m1_copy(w, d).wait_send()
        for a in range(1, 4):
            e2_copy(w, a).wait_send()
        for zz in range(2):
            away, cp = deliver_copy(w, zz)

            @pl.when(away)
            def _():
                cp.wait_send()


def per_device(tokens, scores, expert_ids, slot_expert, w_gate, w_up, w_down):
    vmem = pl.BlockSpec(memory_space=pltpu.VMEM)
    anywhere = pl.BlockSpec(memory_space=pl.ANY)
    dma = pltpu.SemaphoreType.DMA
    return pl.pallas_call(
        kernel,
        out_shape=jax.ShapeDtypeStruct((MB, 4, D), BF16),
        in_specs=[
            anywhere, vmem, vmem, pl.BlockSpec(memory_space=pltpu.SMEM),
            anywhere, anywhere, anywhere,
        ],
        out_specs=vmem,
        scratch_shapes=[
            pltpu.VMEM((MB, ROWS, D), BF16),
            pltpu.VMEM((2, W, H), BF16),
            pltpu.VMEM((H, W), BF16),
            pltpu.VMEM((2, MB, CAP, ROWS), BF16),
            pltpu.VMEM((MB, 6, CAP, W), BF16),
            pltpu.VMEM((MB, 2, NDP, CAP, W), BF16),
            pltpu.VMEM((MB, NDP, 2, CAP, 2 * HQ), F32),
            pltpu.VMEM((2, NCH, CAP, 2 * HQ), BF16),
            pltpu.VMEM((2, NCH, CAP, 2 * HQ), BF16),
            pltpu.VMEM((UNITS, 2, 2, 2, CAP, HQ), BF16),
            pltpu.VMEM((4, 32, W), F32),
            pltpu.VMEM((PIECES, 32, W), F32),
            pltpu.VMEM((PIECES, 2, 16, W), F32),
            pltpu.VMEM((PIECES, 2, 32, W), BF16),
            pltpu.VMEM((PIECES, 2, 32, W), BF16),
            pltpu.VMEM((PIECES, 2, 16, W), BF16),
            pltpu.VMEM((PIECES, 2, 16, W), BF16),
            pltpu.VMEM((PIECES, 4, 8, W), F32),
            pltpu.VMEM((PIECES, 3, 8, W), F32),
            pltpu.VMEM((PIECES, 2, 8, WF), F32),
            pltpu.VMEM((MB, NDP, 2, 8, WF), F32),
            pltpu.VMEM((8, ROWS), F32),
            pltpu.VMEM((NDP, 8, ROWS), F32),
            dma((7,)),
            dma((4,)), dma((4,)),
            dma((7,)), dma((NDP,)),
            dma((MB, 6)), dma((MB, NDP)),
            dma((MB, 6)), dma((MB, NDP)),
            dma((MB,)), dma((MB,)),
            dma((2, NCH)), dma((2, NCH)),
            dma((2, NCH)), dma((2, NCH)),
            dma((2, NCH)), dma((2, NCH)),
            dma((PIECES, 2)), dma((PIECES, 2)),
            dma((PIECES, 2)), dma((PIECES, 2)),
            dma((PIECES, 3)), dma((PIECES, 3)),
            dma((PIECES, 2)), dma((MB, NDP, 2)),
        ],
        compiler_params=pltpu.CompilerParams(
            collective_id=0, has_side_effects=True, vmem_limit_bytes=56 * 2**20
        ),
        name="expert_layer",
    )(
        tokens, jnp.swapaxes(scores, 1, 2), jnp.swapaxes(expert_ids, 1, 2), slot_expert,
        w_gate, w_up, w_down,
    )


def solution(mesh):
    in_specs = (
        P(None, "dp", None),
        P(None, "dp", None),
        P(None, "dp", None),
        P(),
        P("expert", "dp", None),
        P("expert", "dp", None),
        P("expert", None, "dp"),
    )
    out_specs = P(None, ("dp", "expert"), None)
    return jax.shard_map(
        per_device, mesh=mesh, in_specs=in_specs, out_specs=out_specs, check_vma=False
    )
```

time: 115 us -> 95.5 us (0.83); the launches traced: 113 us -> 95.3 us
  Pallas kernels: 109 us -> 93.7 us
  local copies, waits for them, and re-layouts: 4.54 us -> 1.59 us
    pallas_call x1, Pallas kernels: 109 us -> 93.7 us  [per_device(): pl.pallas_call(kernel, out_shape=jax.ShapeDtypeStruct((MB, 4, D), BF16),...]
    reshape x1 -> x0, local copies, waits for them, and re-layouts: 1.6 us -> none  [per_device(): return out.reshape(MB, 4, D)]
    unnamed x2 -> x1, local copies, waits for them, and re-layouts: 2.95 us -> 1.59 us
where the time goes in v2:
time: 95.5 us; the launch traced here: 95.3 us
  Pallas kernels  93.7 us (98%)
  local copies, waits for them, and re-layouts  1.59 us (2%)
    pallas_call x1, Pallas kernels, per_device(): pl.pallas_call(kernel, out_shape=jax.ShapeDtypeStruct((MB, 4, D), BF16),...  93.7 us

profile of v2, /device:TPU:33, one launch (start us, length us, event | category | flops | bytes accessed | tf_op | source)
XLA Modules:
  0.0 95.3 jit_solution(2885017635385311476)
XLA Ops:
  0.0 93.7 %expert_layer.1 = bf16[2,4,7168]{2,1,0:T(4,128)(2,1)} custom-call(bf16[2,128,7168]{2,1,0:T(8,128)(2,1)} %tok_hbm.1, f32[2,8,128]{2,1,0:T(8,128)} %bitcast.2, s32[2,8,128]{2,1,0:T(8,128)} %bitcast.3, s32[32]{0:T(128)} %slot_ref.1, bf16[1,896,1024]{2,1,0:T(8,128)(2,1)} %wg_hbm.1, bf16[1,896,1024]{2,1,0:T(8,128)(2,1)} %wu_hbm.1, bf16[1,1024,896]{2,1,0:T(8,128)(2,1)} %wd_hbm.1), custom_call_target="tpu_custom_call" | custom-call | tf_op jit(solution)/shard_map/expert_layer/pallas_call | solution.py:500
  93.7 1.6 %copy.9 = bf16[2,4,7168]{2,1,0:T(4,128)(2,1)} copy(bf16[2,4,7168]{2,1,0:T(4,128)(2,1)} %expert_layer.1) | data formatting | bytes 229376

commit v3 on v2

--- a/solution.py
+++ b/solution.py
@@ -22,12 +22,13 @@
 NCH = 16
 UNITS = 8
 WF = 512
-SKEW = 3
+MID = 4
+AHEAD = 3
+SKEW = 2
 PIECES = 16
 LAG0 = 6 * SKEW + 2
-LAG1 = LAG0 + 6
-LAG2 = LAG1 + 6
-LAG3 = LAG2 + 6
+LAG1 = LAG0 + 4
+LAG2 = LAG1 + 4
 
 
 def div(a, b):
@@ -40,10 +41,10 @@
 
 def kernel(
     tok_hbm, scores_ref, ids_ref, slot_ref, wg_hbm, wu_hbm, wd_hbm, out_ref,
-    tok, wgu, wd, pick, pk, xin, part, bsend, brecv, hid, zf, zown, keep, e1s, e1r, m1s, m1r, e2s, e2r,
+    tok, wgu, wd, pick, pk, xin, part, bsend, brecv, hid, yv, zf, zown, e1s, e1r, e2f, e2o, e2s, e2r,
     fs, fr, rts, rtr,
     s_loc, s_w, r_w, s_rt, r_rt, s_a, r_a, s_f, r_f, s_o, r_o,
-    s_b, r_b, s_c, r_c, s_p, r_p, s_e1, r_e1, s_m1, r_m1, s_e2, r_e2, s_x, r_x,
+    s_b, r_b, s_c, r_c, s_p, r_p, s_e1, r_e1, s_e2, r_e2, s_x, r_x,
 ):
     dp = lax.axis_index("dp")
     ex = lax.axis_index("expert")
@@ -67,16 +68,6 @@
             src_ref=src, dst_ref=dst, send_sem=ssem, recv_sem=rsem,
             device_id=dev, device_id_type=MESH,
         )
-
-    bar = pltpu.get_barrier_semaphore()
-    for a in range(NDP):
-        for b in range(2):
-            if a or b:
-                dev = (rem(dp + a, NDP), (y * 2 + rem(zh + b, 2)) * 4 + x)
-                pl.semaphore_signal(bar, inc=1, device_id=dev, device_id_type=MESH)
-    for a in range(1, 4):
-        pl.semaphore_signal(bar, inc=1, device_id=xdev(rem(x + a, 4)), device_id_type=MESH)
-        pl.semaphore_signal(bar, inc=1, device_id=ydev(rem(y + a, 4)), device_id_type=MESH)
 
     def hidden_at(core, half):
         return pl.ds(pl.multiple_of(core * HH + half * HQ, 128), HQ)
@@ -95,6 +86,16 @@
     loads.append(pltpu.make_async_copy(wd_hbm.at[0], wd, s_loc.at[6]))
     for cp in loads:
         cp.start()
+
+    bar = pltpu.get_barrier_semaphore()
+    for a in range(NDP):
+        for b in range(2):
+            if a or b:
+                dev = (rem(dp + a, NDP), (y * 2 + rem(zh + b, 2)) * 4 + x)
+                pl.semaphore_signal(bar, inc=1, device_id=dev, device_id_type=MESH)
+    for a in range(1, 4):
+        pl.semaphore_signal(bar, inc=1, device_id=xdev(rem(x + a, 4)), device_id_type=MESH)
+        pl.semaphore_signal(bar, inc=1, device_id=ydev(rem(y + a, 4)), device_id_type=MESH)
 
     row8 = lax.broadcasted_iota(jnp.int32, (8, ROWS), 0)
     rows = jnp.zeros((8, ROWS), F32)
@@ -201,14 +202,14 @@
                 xin.at[mb, c, i], xin.at[mb, oc, i], s_f.at[mb, n], r_f.at[mb, i], peer
             ).wait_recv()
 
-    def project_in(mb, n):
-        at = pl.ds(n * HQ, HQ)
+    def project_in(mb, half):
+        at = pl.ds(half * 2 * HQ, 2 * HQ)
         total = jnp.dot(
             xin[mb, 0].reshape(NDP * CAP, W), wgu[0, :, at], preferred_element_type=F32
         ) + jnp.dot(
             xin[mb, 1].reshape(NDP * CAP, W), wgu[1, :, at], preferred_element_type=F32
         )
-        part[mb, :, n // 2, :, (n % 2) * HQ : (n % 2 + 1) * HQ] = total.reshape(NDP, CAP, HQ)
+        part[mb, :, half] = total.reshape(NDP, CAP, 2 * HQ)
 
     def chain(d, k):
         half, u = rem(k, 2), div(k, 2)
@@ -218,34 +219,34 @@
         down = (dp - 2 if d == 0 else dp + 2, ex)
         slot = hid.at[u, c, half, 1 - d]
         own = part.at[mb, q + 4 * (1 - d), half]
-        sums = remote(bsend.at[d, k], brecv.at[d, k], s_b.at[d, k], r_b.at[d, k], up)
-        relay = remote(slot, slot, s_c.at[d, k], r_c.at[d, k], down)
-        across = remote(slot, slot, s_p.at[d, k], r_p.at[d, k], peer)
+        sums = remote(bsend.at[d, k], brecv.at[d, k], s_b.at[d], r_b.at[d, k], up)
+        relay = remote(slot, slot, s_c.at[d], r_c.at[d, k], down)
+        both = hid.at[u, c, :, 1 - d]
+        across = remote(both, both, s_p.at[d], r_p.at[d, u], peer)
         return own, slot, p, sums, relay, across
+
+    def chain_start(k):
+        for d in range(2):
+
+            @pl.when((zl if d == 0 else 3 - zl) == 0)
+            def _():
+                own, slot, p, sums, relay, across = chain(d, k)
+                bsend[d, k] = own[...].astype(BF16)
+                sums.start()
 
     def chain_step(t):
         for d in range(2):
             p0 = zl if d == 0 else 3 - zl
             k = t - SKEW * p0
 
-            @pl.when((k >= 0) & (k < NCH))
+            @pl.when((p0 > 0) & (k >= 0) & (k < NCH))
             def _():
                 own, slot, p, sums, relay, across = chain(d, k)
-
-                @pl.when(p == 0)
-                def _():
-                    bsend[d, k] = own[...].astype(BF16)
-
-                @pl.when(p > 0)
-                def _():
-                    sums.wait_recv()
-
-                @pl.when((p > 0) & (p < 3))
+                sums.wait_recv()
+
+                @pl.when(p < 3)
                 def _():
                     bsend[d, k] = (own[...] + brecv[d, k].astype(F32)).astype(BF16)
-
-                @pl.when(p < 3)
-                def _():
                     sums.start()
 
                 @pl.when(p == 3)
@@ -254,7 +255,10 @@
                     lift = own[:, HQ : 2 * HQ] + brecv[d, k, :, HQ : 2 * HQ].astype(F32)
                     slot[...] = (gate / (1.0 + jnp.exp(-gate)) * lift).astype(BF16)
                     relay.start()
-                    across.start()
+
+                    @pl.when(rem(k, 2) == 1)
+                    def _():
+                        across.start()
 
         for d in range(2):
             p0 = zl if d == 0 else 3 - zl
@@ -269,69 +273,66 @@
                 def _():
                     relay.start()
 
-                across.start()
+                @pl.when(rem(k2, 2) == 1)
+                def _():
+                    across.start()
 
     def chain_sends():
-        @pl.loop(0, NCH)
-        def _(k):
-            for d in range(2):
-                own, slot, p, sums, relay, across = chain(d, k)
-
-                @pl.when(p < 3)
-                def _():
-                    sums.wait_send()
-
-                @pl.when(p > 0)
-                def _():
-                    relay.wait_send()
-
-                across.wait_send()
+        for d in range(2):
+            p = zl if d == 0 else 3 - zl
+            sent = hid.at[:, c, :, 1 - d]
+
+            @pl.when(p < 3)
+            def _():
+                remote(bsend.at[d], brecv.at[d], s_b.at[d], r_b.at[d, 0], peer).wait_send()
+
+            @pl.when(p > 0)
+            def _():
+                remote(sent, sent, s_c.at[d], r_c.at[d, 0], peer).wait_send()
+
+            remote(sent, sent, s_p.at[d], r_p.at[d, 0], peer).wait_send()
 
     def split(w):
         u, g = div(w, 2), rem(w, 2)
         return u, g, div(u, 4), rem(u, 4)
 
-    def project_out(w):
-        u, g, mb, q = split(w)
-        for half in range(2):
-            there = hid.at[u, oc, half, g]
-            k = u * 2 + half
-            remote(there, there, s_p.at[1 - g, k], r_p.at[1 - g, k], peer).wait_recv()
-        total = jnp.zeros((CAP, W), F32)
+    def project_out(u):
+        for g in range(2):
+            there = hid.at[u, oc, :, g]
+            remote(there, there, s_p.at[1 - g], r_p.at[1 - g, u], peer).wait_recv()
+        total = jnp.zeros((2 * CAP, W), F32)
         for core in range(2):
             for half in range(2):
                 total = total + jnp.dot(
-                    hid[u, core, half, g],
+                    hid[u, core, half].reshape(2 * CAP, HQ),
                     wd[core * HH + half * HQ : core * HH + (half + 1) * HQ],
                     preferred_element_type=F32,
                 )
-        return total.astype(BF16)
-
-    def expert_at(g, a, first):
-        along_x = (g == 0) == first
-        to_x = jnp.where(along_x, rem(x + a, 4), x)
-        to_y = jnp.where(along_x, y, rem(y + a, 4))
-        return (dp, (to_y * 2 + zh) * 4 + to_x)
-
-    def e1_copy(w, d):
-        dev = expert_at(rem(w, 2), 1 if d == 0 else 3, True)
-        return remote(e1s.at[w, d], e1r.at[w, d], s_e1.at[w, d], r_e1.at[w, d], dev)
-
-    def m1_copy(w, d):
-        dev = expert_at(rem(w, 2), 1 if d == 0 else 3, True)
-        return remote(m1s.at[w, d], m1r.at[w, d], s_m1.at[w, d], r_m1.at[w, d], dev)
+        yv[...] = total.astype(BF16).reshape(2, CAP, W)
+
+    to_x = [xdev(rem(x + a, 4)) for a in range(4)]
+    to_y = [ydev(rem(y + a, 4)) for a in range(4)]
+
+    def along(on_x, a):
+        return (dp, jnp.where(on_x, to_x[a][1], to_y[a][1]))
+
+    def e1_copy(w, a):
+        g = rem(w, 2)
+        to = rem(jnp.where(g == 0, x, y) + a, 4)
+        return remote(e1s.at[w, to], e1r.at[w, a - 1], s_e1, r_e1.at[w], along(g == 0, a))
 
     def e2_copy(w, a):
         g = rem(w, 2)
         to = rem(jnp.where(g == 0, y, x) + a, 4)
-        dev = expert_at(g, a, False)
-        return remote(
-            e2s.at[w, to], e2r.at[w, a - 1], s_e2.at[w, a - 1], r_e2.at[w, a - 1], dev
-        )
+        return remote(e2s.at[w, to], e2r.at[w, a - 1], s_e2, r_e2.at[w], along(g == 1, a))
 
     def spread(w):
         u, g, mb, q = split(w)
-        rows_out = project_out(w)
+
+        @pl.when(g == 0)
+        def _():
+            project_out(u)
+
         spot = lax.broadcasted_iota(jnp.int32, (ROWS, CAP), 1).astype(F32)
         row = lax.broadcasted_iota(jnp.int32, (8, ROWS), 0)
         told = rtr[g * 4 + q]
@@ -339,34 +340,25 @@
         share = jnp.sum(jnp.where(row == zh * 4 + 2 + mb, told, 0.0), axis=0, keepdims=True)
         turned = jnp.transpose(jnp.where(row == 0, rank, share))
         one = jnp.where(turned[:, 0:1] == spot, 1.0, 0.0).astype(BF16)
-        value = turned[:, 1:2] * jnp.dot(one, rows_out, preferred_element_type=F32)
+        value = turned[:, 1:2] * jnp.dot(one, yv[g], preferred_element_type=F32)
         zf[...] = value.reshape(4, 32, W)
-        at = jnp.where(g == 0, x, y)
-        above, far, below = rem(at + 1, 4), rem(at + 2, 4), rem(at + 3, 4)
-        e1s[w, 0, 0:16] = zf[far, 0:16].astype(BF16)
-        e1s[w, 0, 16:32] = zf[above, 16:32].astype(BF16)
-        e1s[w, 1, 0:16] = zf[far, 16:32].astype(BF16)
-        e1s[w, 1, 16:32] = zf[below, 0:16].astype(BF16)
-        for d in range(2):
-            e1_copy(w, d).start()
-        keep[w, 0] = zf[above, 0:16]
-        keep[w, 1] = zf[below, 16:32]
-        zown[w] = zf[at]
-
-    def merge(w):
-        for d in range(2):
-            e1_copy(w, d).wait_recv()
-            m1s[w, d] = (keep[w, d] + e1r[w, d, 0:16].astype(F32)).astype(BF16)
-            m1_copy(w, d).start()
+        e1s[w] = zf[...].astype(BF16)
+        for a in (2, 1, 3):
+            e1_copy(w, a).start()
+        zown[w] = zf[jnp.where(g == 0, x, y)]
 
     def combine1(w):
-        for d in range(2):
-            m1_copy(w, d).wait_recv()
+        remote(e1s.at[w, 0:3], e1r.at[w], s_e1, r_e1.at[w], peer).wait_recv()
         for d in range(2):
             rows = slice(16 * d, 16 * d + 16)
-            total = zown[w, rows] + e1r[w, 1 - d, 16:32].astype(F32)
-            total = total + m1r[w, d].astype(F32)
-            e2s[w, 2 * d : 2 * d + 2] = total.reshape(2, 8, W)
+            total = zown[w, rows]
+            for a in range(3):
+                total = total + e1r[w, a, rows].astype(F32)
+            for b in range(2):
+                e2f[2 * d + b, 0:8] = total[8 * b : 8 * b + 8, 0:WF]
+                e2f[2 * d + b, 8:16, 0 : W - WF] = total[8 * b : 8 * b + 8, WF:W]
+        e2s[w] = e2f[...].astype(BF16)
+        e2o[w] = e2f[jnp.where(rem(w, 2) == 0, y, x)]
         for a in (2, 1, 3):
             e2_copy(w, a).start()
 
@@ -376,19 +368,17 @@
         dev = (i, (y * 2 + zz) * 4 + x)
         away = (i != dp) | (zh != zz)
         return away, remote(
-            fs.at[w, zz], fr.at[mb, dp, zh], s_x.at[w, zz], r_x.at[mb, dp, zh], dev
+            fs.at[w, zz], fr.at[mb, dp * 2 + zh], s_x, r_x.at[mb], dev
         )
 
     def combine2(w):
         u, g, mb, q = split(w)
         top = lax.broadcasted_iota(jnp.int32, (8, WF), 0) < 4
-        for a in (1, 3, 2):
-            e2_copy(w, a).wait_recv()
-        total = e2s[w, jnp.where(g == 0, y, x)]
+        remote(e2s.at[w, 0:3], e2r.at[w], s_e2, r_e2.at[w], peer).wait_recv()
+        total = e2o[w]
         for a in range(3):
-            total = total + e2r[w, a]
-        lo = total[:, 0:WF]
-        hi = jnp.concatenate([total[:, WF:W], jnp.zeros((8, 2 * WF - W), F32)], axis=1)
+            total = total + e2r[w, a].astype(F32)
+        lo, hi = total[0:8], total[8:16]
         fs[w, 0] = jnp.where(top, lo, pltpu.roll(hi, 4, 0))
         fs[w, 1] = jnp.where(top, pltpu.roll(lo, 4, 0), hi)
         for zz in range(2):
@@ -400,18 +390,18 @@
 
             @pl.when(jnp.logical_not(away))
             def _():
-                fr[mb, dp, zh] = fs[w, zz]
+                fr[mb, dp * 2 + zh] = fs[w, zz]
+
+    def combine_sends():
+        remote(e1s.at[:, 0:3], e1r, s_e1, r_e1.at[0], peer).wait_send()
+        remote(e2s.at[:, 0:3], e2r, s_e2, r_e2.at[0], peer).wait_send()
+        remote(fs.at[0:15], fs.at[0:15], s_x, r_x.at[0], peer).wait_send()
 
     def finish(mb):
-        for a in range(NDP):
-            for b in range(2):
-                if a or b:
-                    j, zz = rem(dp + NDP - a, NDP), rem(zh + b, 2)
-                    remote(
-                        fs.at[0, 0], fr.at[mb, j, zz], s_x.at[0, 0], r_x.at[mb, j, zz], peer
-                    ).wait_recv()
+        there = fr.at[mb, 0:15]
+        remote(there, there, s_x, r_x.at[mb], peer).wait_recv()
         for j in range(NDP):
-            total = (fr[mb, j, 0] + fr[mb, j, 1]).astype(BF16)
+            total = (fr[mb, 2 * j] + fr[mb, 2 * j + 1]).astype(BF16)
             out_ref[mb, :, j * W : j * W + WF] = total[0:4]
             out_ref[mb, :, j * W + WF : (j + 1) * W] = total[4:8, 0 : W - WF]
 
@@ -422,6 +412,7 @@
     loads[1].wait()
     dispatch(1)
     announce()
+    e2f[...] = jnp.zeros((4, 16, WF), F32)
     for k in range(4):
         loads[2 + k].wait()
     for k in range(4):
@@ -430,37 +421,45 @@
             ref.at[0, :, hidden_at(oc, k // 2)], wgu.at[oc, :, at], s_w.at[k], r_w.at[k], peer
         ).wait_recv()
     collect(0)
-    for n in range(4):
-        project_in(0, n)
-
-    @pl.loop(0, 4)
-    def _(t):
+    project_in(0, 0)
+    chain_start(0)
+    project_in(0, 1)
+
+    @pl.loop(1, NCH // 2)
+    def _(k):
+        chain_start(k)
+
+    for t in range(1, MID + 4):
         chain_step(t)
-
-    collect(1)
-    for n in range(4):
-        chain_step(4 + n)
-        project_in(1, n)
+        if t == MID:
+            collect(1)
+        if t in (MID, MID + 2):
+            project_in(1, (t - MID) // 2)
+
+    @pl.loop(NCH // 2, NCH // 2 + AHEAD)
+    def _(k):
+        chain_start(k)
+
     loads[6].wait()
     for n in range(6):
         remote(rts, rtr.at[source[n]], s_rt.at[n], r_rt.at[source[n]], peer).wait_recv()
     remote(rts, rtr.at[zl * 2 + oc], s_rt.at[6], r_rt.at[zl * 2 + oc], peer).wait_recv()
 
-    @pl.loop(8, PIECES + LAG3)
+    @pl.loop(MID + 4, PIECES + LAG2)
     def _(t):
         chain_step(t)
 
-        @pl.when(t >= LAG3)
+        @pl.when(t < NCH // 2 - AHEAD + MID + 4)
         def _():
-            combine2(t - LAG3)
-
-        @pl.when((t >= LAG2) & (t < LAG2 + PIECES))
+            chain_start(t + NCH // 2 + AHEAD - MID - 4)
+
+        @pl.when(t >= LAG2)
         def _():
-            combine1(t - LAG2)
+            combine2(t - LAG2)
 
         @pl.when((t >= LAG1) & (t < LAG1 + PIECES))
         def _():
-            merge(t - LAG1)
+            combine1(t - LAG1)
 
         @pl.when((t >= LAG0) & (t < LAG0 + PIECES))
         def _():
@@ -469,28 +468,15 @@
     finish(0)
     finish(1)
 
+    chain_sends()
+    combine_sends()
     for cp in weight_copies() + info_copies():
         cp.wait_send()
-    chain_sends()
     for mb in range(MB):
         own_copy(mb).wait_send()
         for n in range(6):
             piece_copy(mb, n).wait_send()
             forward_copy(mb, n).wait_send()
-
-    @pl.loop(0, PIECES)
-    def _(w):
-        for d in range(2):
-            e1_copy(w, d).wait_send()
-            m1_copy(w, d).wait_send()
-        for a in range(1, 4):
-            e2_copy(w, a).wait_send()
-        for zz in range(2):
-            away, cp = deliver_copy(w, zz)
-
-            @pl.when(away)
-            def _():
-                cp.wait_send()
 
 
 def per_device(tokens, scores, expert_ids, slot_expert, w_gate, w_up, w_down):
@@ -516,17 +502,17 @@
             pltpu.VMEM((2, NCH, CAP, 2 * HQ), BF16),
             pltpu.VMEM((2, NCH, CAP, 2 * HQ), BF16),
             pltpu.VMEM((UNITS, 2, 2, 2, CAP, HQ), BF16),
+            pltpu.VMEM((2, CAP, W), BF16),
             pltpu.VMEM((4, 32, W), F32),
             pltpu.VMEM((PIECES, 32, W), F32),
-            pltpu.VMEM((PIECES, 2, 16, W), F32),
-            pltpu.VMEM((PIECES, 2, 32, W), BF16),
-            pltpu.VMEM((PIECES, 2, 32, W), BF16),
-            pltpu.VMEM((PIECES, 2, 16, W), BF16),
-            pltpu.VMEM((PIECES, 2, 16, W), BF16),
-            pltpu.VMEM((PIECES, 4, 8, W), F32),
-            pltpu.VMEM((PIECES, 3, 8, W), F32),
+            pltpu.VMEM((PIECES, 4, 32, W), BF16),
+            pltpu.VMEM((PIECES, 3, 32, W), BF16),
+            pltpu.VMEM((4, 16, WF), F32),
+            pltpu.VMEM((PIECES, 16, WF), F32),
+            pltpu.VMEM((PIECES, 4, 16, WF), BF16),
+            pltpu.VMEM((PIECES, 3, 16, WF), BF16),
             pltpu.VMEM((PIECES, 2, 8, WF), F32),
-            pltpu.VMEM((MB, NDP, 2, 8, WF), F32),
+            pltpu.VMEM((MB, 2 * NDP, 8, WF), F32),
             pltpu.VMEM((8, ROWS), F32),
             pltpu.VMEM((NDP, 8, ROWS), F32),
             dma((7,)),
@@ -535,13 +521,12 @@
             dma((MB, 6)), dma((MB, NDP)),
             dma((MB, 6)), dma((MB, NDP)),
             dma((MB,)), dma((MB,)),
-            dma((2, NCH)), dma((2, NCH)),
-            dma((2, NCH)), dma((2, NCH)),
-            dma((2, NCH)), dma((2, NCH)),
-            dma((PIECES, 2)), dma((PIECES, 2)),
-            dma((PIECES, 2)), dma((PIECES, 2)),
-            dma((PIECES, 3)), dma((PIECES, 3)),
-            dma((PIECES, 2)), dma((MB, NDP, 2)),
+            dma((2,)), dma((2, NCH)),
+            dma((2,)), dma((2, NCH)),
+            dma((2,)), dma((2, UNITS)),
+            dma, dma((PIECES,)),
+            dma, dma((PIECES,)),
+            dma, dma((MB,)),
         ],
         compiler_params=pltpu.CompilerParams(
             collective_id=0, has_side_effects=True, vmem_limit_bytes=56 * 2**20

time: 95.5 us -> 90.7 us (0.950)
  Pallas kernels: 93.7 us -> 89 us
    pallas_call x1, Pallas kernels: 93.7 us -> 89 us  [per_device(): pl.pallas_call(kernel, out_shape=jax.ShapeDtypeStruct((MB, 4, D), BF16),...]
where the time goes in v3:
time: 90.7 us; the launch traced here: 90.6 us
  Pallas kernels  89 us (98%)
  local copies, waits for them, and re-layouts  1.59 us (2%)
    pallas_call x1, Pallas kernels, per_device(): pl.pallas_call(kernel, out_shape=jax.ShapeDtypeStruct((MB, 4, D), BF16),...  89 us

profile of v3, /device:TPU:33, one launch (start us, length us, event | category | flops | bytes accessed | tf_op | source)
XLA Modules:
  0.0 90.6 jit_solution(4813180097555816510)
XLA Ops:
  0.0 89.0 %expert_layer.1 = bf16[2,4,7168]{2,1,0:T(4,128)(2,1)} custom-call(bf16[2,128,7168]{2,1,0:T(8,128)(2,1)} %tok_hbm.1, f32[2,8,128]{2,1,0:T(8,128)} %bitcast.2, s32[2,8,128]{2,1,0:T(8,128)} %bitcast.3, s32[32]{0:T(128)} %slot_ref.1, bf16[1,896,1024]{2,1,0:T(8,128)(2,1)} %wg_hbm.1, bf16[1,896,1024]{2,1,0:T(8,128)(2,1)} %wu_hbm.1, bf16[1,1024,896]{2,1,0:T(8,128)(2,1)} %wd_hbm.1), custom_call_target="tpu_custom_call" | custom-call | tf_op jit(solution)/shard_map/expert_layer/pallas_call | solution.py:486
  89.0 1.6 %copy.9 = bf16[2,4,7168]{2,1,0:T(4,128)(2,1)} copy(bf16[2,4,7168]{2,1,0:T(4,128)(2,1)} %expert_layer.1) | data formatting | bytes 229376

commit v4 on v3

--- a/solution.py
+++ b/solution.py
@@ -24,9 +24,10 @@
 WF = 512
 MID = 4
 AHEAD = 3
-SKEW = 2
+SKEW = 3
+BACK = 2
 PIECES = 16
-LAG0 = 6 * SKEW + 2
+LAG0 = 3 * (SKEW + BACK) + 1
 LAG1 = LAG0 + 4
 LAG2 = LAG1 + 4
 
@@ -204,10 +205,9 @@
 
     def project_in(mb, half):
         at = pl.ds(half * 2 * HQ, 2 * HQ)
+        rows_in = jnp.concatenate([xin[mb, k].reshape(NDP * CAP, W) for k in range(2)], axis=1)
         total = jnp.dot(
-            xin[mb, 0].reshape(NDP * CAP, W), wgu[0, :, at], preferred_element_type=F32
-        ) + jnp.dot(
-            xin[mb, 1].reshape(NDP * CAP, W), wgu[1, :, at], preferred_element_type=F32
+            rows_in, wgu[:, :, at].reshape(2 * W, 2 * HQ), preferred_element_type=F32
         )
         part[mb, :, half] = total.reshape(NDP, CAP, 2 * HQ)
 
@@ -262,7 +262,7 @@
 
         for d in range(2):
             p0 = zl if d == 0 else 3 - zl
-            k2 = t - SKEW * (6 - p0)
+            k2 = t - 3 * SKEW - BACK * (3 - p0)
 
             @pl.when((p0 < 3) & (k2 >= 0) & (k2 < NCH))
             def _():
@@ -300,14 +300,10 @@
         for g in range(2):
             there = hid.at[u, oc, :, g]
             remote(there, there, s_p.at[1 - g], r_p.at[1 - g, u], peer).wait_recv()
-        total = jnp.zeros((2 * CAP, W), F32)
-        for core in range(2):
-            for half in range(2):
-                total = total + jnp.dot(
-                    hid[u, core, half].reshape(2 * CAP, HQ),
-                    wd[core * HH + half * HQ : core * HH + (half + 1) * HQ],
-                    preferred_element_type=F32,
-                )
+        parts = [hid[u, core, half].reshape(2 * CAP, HQ) for core in range(2) for half in range(2)]
+        total = jnp.dot(
+            jnp.concatenate(parts, axis=1), wd[...], preferred_element_type=F32
+        )
         yv[...] = total.astype(BF16).reshape(2, CAP, W)
 
     to_x = [xdev(rem(x + a, 4)) for a in range(4)]
@@ -341,8 +337,9 @@
         turned = jnp.transpose(jnp.where(row == 0, rank, share))
         one = jnp.where(turned[:, 0:1] == spot, 1.0, 0.0).astype(BF16)
         value = turned[:, 1:2] * jnp.dot(one, yv[g], preferred_element_type=F32)
-        zf[...] = value.reshape(4, 32, W)
-        e1s[w] = zf[...].astype(BF16)
+        value = value.reshape(4, 32, W)
+        e1s[w] = value.astype(BF16)
+        zf[...] = value
         for a in (2, 1, 3):
             e1_copy(w, a).start()
         zown[w] = zf[jnp.where(g == 0, x, y)]

time: 90.7 us -> 89.6 us (0.988)
  Pallas kernels: 89 us -> 87.8 us
    pallas_call x1, Pallas kernels: 89 us -> 87.8 us  [per_device(): pl.pallas_call(kernel, out_shape=jax.ShapeDtypeStruct((MB, 4, D), BF16),...]
where the time goes in v4:
time: 89.6 us; the launch traced here: 89.4 us
  Pallas kernels  87.8 us (98%)
  local copies, waits for them, and re-layouts  1.59 us (2%)
    pallas_call x1, Pallas kernels, per_device(): pl.pallas_call(kernel, out_shape=jax.ShapeDtypeStruct((MB, 4, D), BF16),...  87.8 us

profile of v4, /device:TPU:33, one launch (start us, length us, event | category | flops | bytes accessed | tf_op | source)
XLA Modules:
  0.0 89.4 jit_solution(1858688837366026039)
XLA Ops:
  0.0 87.8 %expert_layer.1 = bf16[2,4,7168]{2,1,0:T(4,128)(2,1)} custom-call(bf16[2,128,7168]{2,1,0:T(8,128)(2,1)} %tok_hbm.1, f32[2,8,128]{2,1,0:T(8,128)} %bitcast.2, s32[2,8,128]{2,1,0:T(8,128)} %bitcast.3, s32[32]{0:T(128)} %slot_ref.1, bf16[1,896,1024]{2,1,0:T(8,128)(2,1)} %wg_hbm.1, bf16[1,896,1024]{2,1,0:T(8,128)(2,1)} %wu_hbm.1, bf16[1,1024,896]{2,1,0:T(8,128)(2,1)} %wd_hbm.1), custom_call_target="tpu_custom_call" | custom-call | tf_op jit(solution)/shard_map/expert_layer/pallas_call | solution.py:483
  87.8 1.6 %copy.9 = bf16[2,4,7168]{2,1,0:T(4,128)(2,1)} copy(bf16[2,4,7168]{2,1,0:T(4,128)(2,1)} %expert_layer.1) | data formatting | bytes 229376

commit v5 on v4

--- a/solution.py
+++ b/solution.py
@@ -134,13 +134,13 @@
 
     def piece_copy(mb, n):
         return remote(
-            pk.at[mb, n], xin.at[mb, n % 2, dp], s_a.at[mb, n], r_a.at[mb, dp],
+            pk.at[mb, n], xin.at[mb, n % 2, dp], s_a.at[mb], r_a.at[mb, dp],
             column(dest_z[n], n % 2),
         )
 
     def forward_copy(mb, n):
         i = source[n]
-        return remote(xin.at[mb, c, i], xin.at[mb, c, i], s_f.at[mb, n], r_f.at[mb, i], peer)
+        return remote(xin.at[mb, c, i], xin.at[mb, c, i], s_f.at[mb], r_f.at[mb], peer)
 
     def own_copy(mb):
         return remote(xin.at[mb, :, dp], xin.at[mb, :, dp], s_o.at[mb], r_o.at[mb], peer)
@@ -159,10 +159,10 @@
 
     def info_copies():
         out = [
-            remote(rts, rtr.at[dp], s_rt.at[n], r_rt.at[dp], column(dest_z[n], n % 2))
+            remote(rts, rtr.at[dp], s_rt, r_rt, column(dest_z[n], n % 2))
             for n in range(6)
         ]
-        return out + [remote(rts, rtr.at[dp], s_rt.at[6], r_rt.at[dp], peer)]
+        return out + [remote(rts, rtr.at[dp], s_rt, r_rt, peer)]
 
     def dispatch(mb):
         for n in range(6):
@@ -190,18 +190,15 @@
         for n in (2, 3, 4, 5, 0, 1):
             i = source[n]
             remote(
-                pk.at[mb, n], xin.at[mb, c, i], s_a.at[mb, n], r_a.at[mb, i], peer
+                pk.at[mb, n], xin.at[mb, c, i], s_a.at[mb], r_a.at[mb, i], peer
             ).wait_recv()
             forward_copy(mb, n).start()
         own = remote(
             xin.at[mb, :, dp], xin.at[mb, :, zl * 2 + oc], s_o.at[mb], r_o.at[mb], peer
         )
         own.wait_recv()
-        for n in (2, 3, 4, 5, 0, 1):
-            i = source[n]
-            remote(
-                xin.at[mb, c, i], xin.at[mb, oc, i], s_f.at[mb, n], r_f.at[mb, i], peer
-            ).wait_recv()
+        six = xin.at[mb, oc, 0:6]
+        remote(six, six, s_f.at[mb], r_f.at[mb], peer).wait_recv()
 
     def project_in(mb, half):
         at = pl.ds(half * 2 * HQ, 2 * HQ)
@@ -438,9 +435,17 @@
         chain_start(k)
 
     loads[6].wait()
-    for n in range(6):
-        remote(rts, rtr.at[source[n]], s_rt.at[n], r_rt.at[source[n]], peer).wait_recv()
-    remote(rts, rtr.at[zl * 2 + oc], s_rt.at[6], r_rt.at[zl * 2 + oc], peer).wait_recv()
+    tiles = remote(rtr.at[0:7], rtr.at[0:7], s_rt, r_rt, peer)
+    tiles.wait_recv()
+
+    tiles.wait_send()
+    for cp in weight_copies():
+        cp.wait_send()
+    for mb in range(MB):
+        own_copy(mb).wait_send()
+        remote(pk.at[mb], pk.at[mb], s_a.at[mb], r_a.at[mb, 0], peer).wait_send()
+        six = xin.at[mb, c, 0:6]
+        remote(six, six, s_f.at[mb], r_f.at[mb], peer).wait_send()
 
     @pl.loop(MID + 4, PIECES + LAG2)
     def _(t):
@@ -454,6 +459,10 @@
         def _():
             combine2(t - LAG2)
 
+        @pl.when(t == PIECES + LAG2 - 1)
+        def _():
+            finish(0)
+
         @pl.when((t >= LAG1) & (t < LAG1 + PIECES))
         def _():
             combine1(t - LAG1)
@@ -462,18 +471,9 @@
         def _():
             spread(t - LAG0)
 
-    finish(0)
-    finish(1)
-
     chain_sends()
     combine_sends()
-    for cp in weight_copies() + info_copies():
-        cp.wait_send()
-    for mb in range(MB):
-        own_copy(mb).wait_send()
-        for n in range(6):
-            piece_copy(mb, n).wait_send()
-            forward_copy(mb, n).wait_send()
+    finish(1)
 
 
 def per_device(tokens, scores, expert_ids, slot_expert, w_gate, w_up, w_down):
@@ -514,9 +514,9 @@
             pltpu.VMEM((NDP, 8, ROWS), F32),
             dma((7,)),
             dma((4,)), dma((4,)),
-            dma((7,)), dma((NDP,)),
-            dma((MB, 6)), dma((MB, NDP)),
-            dma((MB, 6)), dma((MB, NDP)),
+            dma, dma,
+            dma((MB,)), dma((MB, NDP)),
+            dma((MB,)), dma((MB,)),
             dma((MB,)), dma((MB,)),
             dma((2,)), dma((2, NCH)),
             dma((2,)), dma((2, NCH)),

time: 89.6 us -> 89.1 us (level)
  no operation moved by 1% of the time
where the time goes in v5:
time: 89.1 us; the launch traced here: 88.9 us
  Pallas kernels  87.4 us (98%)
  local copies, waits for them, and re-layouts  1.59 us (2%)
    pallas_call x1, Pallas kernels, per_device(): pl.pallas_call(kernel, out_shape=jax.ShapeDtypeStruct((MB, 4, D), BF16),...  87.4 us

profile of v5, /device:TPU:33, one launch (start us, length us, event | category | flops | bytes accessed | tf_op | source)
XLA Modules:
  0.0 88.9 jit_solution(5378706815034525250)
XLA Ops:
  0.0 87.4 %expert_layer.1 = bf16[2,4,7168]{2,1,0:T(4,128)(2,1)} custom-call(bf16[2,128,7168]{2,1,0:T(8,128)(2,1)} %tok_hbm.1, f32[2,8,128]{2,1,0:T(8,128)} %bitcast.2, s32[2,8,128]{2,1,0:T(8,128)} %bitcast.3, s32[32]{0:T(128)} %slot_ref.1, bf16[1,896,1024]{2,1,0:T(8,128)(2,1)} %wg_hbm.1, bf16[1,896,1024]{2,1,0:T(8,128)(2,1)} %wu_hbm.1, bf16[1,1024,896]{2,1,0:T(8,128)(2,1)} %wd_hbm.1), custom_call_target="tpu_custom_call" | custom-call | tf_op jit(solution)/shard_map/expert_layer/pallas_call | solution.py:483
  87.4 1.6 %copy.9 = bf16[2,4,7168]{2,1,0:T(4,128)(2,1)} copy(bf16[2,4,7168]{2,1,0:T(4,128)(2,1)} %expert_layer.1) | data formatting | bytes 229376
